TPU v7x, 32 devices: a whole 2x2x4 slice. The times are simulated.
32 devices in a mesh: tile: 8 (over z, x), wp: 4 (over y, core).
Axes of the slice: x: 2, y: 2, z: 4, core: 2. Of those that a mesh axis runs over, the one named last changes fastest.
Arguments:
- visibilities: float32 [8192, 2, 128], P(('tile', 'wp')), may hold values from -6 to 6
- vis_weight: float32 [8192, 128], P(('tile', 'wp')), may hold values from 0.2 to 5
- cell_index: int32 [8192, 128], P(('tile', 'wp')), may hold values from 0 to 4095
- tap_offsets: int32 [8192, 128], P(('tile', 'wp')), may hold values from 0 to 255
- routes: int32 [8192, 1], P(('tile', 'wp')), may hold values from 0 to 31; in each aligned block of 256 rows (0 to 255, 256 to 511, ...) at most 16 rows name the same one
- patch_index: int32 [8192], P(('tile', 'wp')), may hold values from 0 to 255
- kernel: float32 [16, 8], replicated, may hold values from 0.1 to 1
Outputs:
- uv_grid: float32 [4, 8, 2, 1024, 1024], P('wp', 'tile')
Inputs may be any that keep to these rules, and one draw needn't show every extreme that they name: `routes`: the 256 blocks of one device name no value more than 16 times, a bound that some block reaches.
All inputs are finite; a program needn't handle non-finite values.
Results may differ from a plain program's by a relative error of at most 0.0003.
Values sent between devices are 32-bit elements; how exact they have to be, the bound alone decides.
No kernel may reach another device: no remote copies, remote signals or barrier semaphores. Data moves between devices by JAX's collectives and lax.ppermute only.
A program may use at most 192 MiB of HBM per device.

v0:
```python
import jax
import jax.numpy as jnp
from jax import lax
from jax.sharding import PartitionSpec as P

TCOLS = 8
SUB = 64
KW = 8
OVER = 16
TILE = 1024


highest = lax.Precision.HIGHEST


def shifted(block, axis, distance):
    devices = range(lax.axis_size(axis))
    route = [(i - distance, i) for i in devices if i - distance in devices]
    return lax.ppermute(block, axis, route)


def kernel_taps(level_index, kernel):
    level_ids = lax.broadcasted_iota(
        jnp.int32, level_index.shape + (kernel.shape[0],), level_index.ndim
    )
    one_hot = jnp.where(level_index[..., None] == level_ids, 1.0, 0.0).astype(jnp.float32)
    return jnp.einsum("bro,ok->brk", one_hot, kernel, precision=highest)


def spread_matrix(first_cell, taps):
    extent = SUB + KW
    places = lax.broadcasted_iota(jnp.int32, first_cell.shape + (extent,), first_cell.ndim)
    matrix = jnp.zeros(first_cell.shape + (extent,), jnp.float32)
    for tap_index in range(KW):
        matrix = matrix + jnp.where(
            places == first_cell[..., None] + tap_index, taps[..., tap_index : tap_index + 1], 0.0
        )
    return matrix


def unfold_edges(patches):
    leading = patches.shape[:-2]
    block_count = patches.shape[-2]
    padding_keep = [(0, 0)] * len(leading)
    core_part = patches[..., :SUB].reshape(leading + (block_count * SUB,))
    core_part = jnp.pad(core_part, padding_keep + [(0, KW)])
    edge_part = jnp.pad(patches[..., SUB:], padding_keep + [(0, 0), (0, SUB - KW)])
    edge_part = edge_part.reshape(leading + (block_count * SUB,))
    edge_part = jnp.pad(edge_part, padding_keep + [(SUB, 0)])[..., : block_count * SUB + KW]
    return core_part + edge_part


def shards(visibilities, vis_weight, cell_index, tap_offsets, routes, patch_index, kernel):
    blocks = visibilities.shape[0]
    tile_count = lax.axis_size("tile")
    plane_count = lax.axis_size("wp")
    peer_count = tile_count * plane_count
    capacity = max(2, 2 * blocks // peer_count)
    levels = OVER * OVER
    target = routes[:, 0]
    earlier = lax.broadcasted_iota(jnp.int32, (blocks, blocks), 1) < lax.broadcasted_iota(
        jnp.int32, (blocks, blocks), 0
    )
    matches = (target[:, None] == target[None, :]) & earlier
    order_in = jnp.sum(matches.astype(jnp.int32), axis=1)
    slot_index = target * capacity + order_in

    def bucket(values):
        buffer = jnp.zeros((peer_count * capacity,) + values.shape[1:], values.dtype)
        buffer = buffer.at[slot_index].set(values)
        return buffer.reshape((tile_count, plane_count, capacity) + values.shape[1:])

    float_part = visibilities * vis_weight[:, None, :]
    int_part = (cell_index * levels + tap_offsets)[:, None, :]
    sent_float = bucket(float_part)
    sent_ints = bucket(int_part)
    sent_patch = bucket(patch_index)
    arrived = (
        lax.all_to_all(
            lax.all_to_all(sent_float, "tile", split_axis=0, concat_axis=0, tiled=True),
            "wp",
            split_axis=1,
            concat_axis=1,
            tiled=True,
        ),
        lax.all_to_all(
            lax.all_to_all(sent_ints, "tile", split_axis=0, concat_axis=0, tiled=True),
            "wp",
            split_axis=1,
            concat_axis=1,
            tiled=True,
        ),
        lax.all_to_all(
            lax.all_to_all(sent_patch, "tile", split_axis=0, concat_axis=0, tiled=True),
            "wp",
            split_axis=1,
            concat_axis=1,
            tiled=True,
        ),
    )
    got_float, got_ints, got_patch = arrived
    slot_total = peer_count * capacity
    got_float = got_float.reshape((slot_total,) + got_float.shape[3:])
    got_ints = got_ints.reshape((slot_total,) + got_ints.shape[3:])
    got_patch = got_patch.reshape((slot_total,))
    got_cells = got_ints[:, 0] // levels
    got_offsets = got_ints[:, 0] % levels
    patches_across = TILE // SUB
    extent = SUB + KW
    batch_size = min(128, slot_total)
    patch_ids = lax.broadcasted_iota(jnp.int32, (1, patches_across * patches_across), 1)
    patch_list = []
    for first_slot in range(0, slot_total, batch_size):
        last_slot = first_slot + batch_size
        scaled = got_float[first_slot:last_slot]
        batch_cells = got_cells[first_slot:last_slot]
        batch_offsets = got_offsets[first_slot:last_slot]
        rows_along_u = spread_matrix(batch_cells // SUB, kernel_taps(batch_offsets // OVER, kernel))
        rows_along_v = spread_matrix(batch_cells % SUB, kernel_taps(batch_offsets % OVER, kernel))
        weighted = rows_along_u[:, None, :, :] * scaled[:, :, :, None]
        patches = jnp.einsum("bcru,brv->bcuv", weighted, rows_along_v, precision=highest)
        patch_list.append(patches.reshape(batch_size, -1))
    all_patches = jnp.concatenate(patch_list, axis=0)
    chosen = jnp.where(got_patch[:, None] == patch_ids, 1.0, 0.0).astype(jnp.float32)
    accum = jnp.einsum("bs,bx->sx", chosen, all_patches, precision=highest)
    patch_grid = accum.reshape(patches_across, patches_across, 2, extent, extent)
    along_v = unfold_edges(jnp.transpose(patch_grid, (2, 0, 3, 1, 4)))
    along_u = unfold_edges(jnp.transpose(along_v, (0, 3, 1, 2)))
    full_tile = jnp.transpose(along_u, (0, 2, 1))
    tile_place = lax.axis_index("tile")
    leftmost = tile_place % TCOLS == 0
    right_edge = jnp.swapaxes(full_tile[:, :TILE, TILE:], 1, 2)
    from_left = shifted(right_edge, "tile", 1)
    from_left = jnp.where(leftmost, 0.0, from_left)
    lower_edge = full_tile[:, TILE:, :TILE]
    from_above = shifted(lower_edge, "tile", TCOLS)
    corner_edge = full_tile[:, TILE:, TILE:]
    from_corner = shifted(corner_edge, "tile", TCOLS + 1)
    from_corner = jnp.where(leftmost, 0.0, from_corner)
    own_tile = full_tile[:, :TILE, :TILE]
    own_tile = own_tile.at[:, :, :KW].add(jnp.swapaxes(from_left, 1, 2))
    own_tile = own_tile.at[:, :KW, :].add(from_above)
    own_tile = own_tile.at[:, :KW, :KW].add(from_corner)
    return own_tile.reshape(1, 1, 2, TILE, TILE)


def solution(mesh):
    in_specs = (
        P(("tile", "wp"), None, None),
        P(("tile", "wp"), None),
        P(("tile", "wp"), None),
        P(("tile", "wp"), None),
        P(("tile", "wp"), None),
        P(("tile", "wp")),
        P(),
    )
    out_specs = P("wp", "tile", None, None, None)
    return jax.shard_map(shards, mesh=mesh, in_specs=in_specs, out_specs=out_specs, check_vma=False)
```

profile of v0, /device:TPU:0, one launch (start us, length us, event | category | flops | bytes accessed | tf_op | source)
XLA Modules:
  0.0 462.7 jit_solution(4096720146598164027)
XLA Ops:
  1.6 1.6 scatter_custom_fusion
  3.9 7.3 %all-to-all-start = ((s32[8,4,16]{2,1,0:T(4,128)}), s32[8,4,16]{2,1,0:T(4,128)S(1)}, u32[]{:S(2)}, u32[]{:S(2)}) async-start(s32[8,4,16]{2,1,0:T(4,128)} %reshape.419), calls=%async_computation | async-start | bytes 32768 | tf_op jit(solution)/shard_map/all_to_all | solution.py:94
  11.1 2.3 scatter_custom_fusion.1
  13.4 4.3 all-to-all-done
  17.7 3.4 all-to-all-start.2
  21.8 7.5 %all-to-all-done.2 = s32[8,4,16,1,128]{4,2,1,3,0:T(8,128)S(1)} async-done(((s32[8,4,16,1,128]{4,2,1,3,0:T(8,128)}), s32[8,4,16,1,128]{4,2,1,3,0:T(8,128)S(1)}, u32[]{:S(2)}, u32[]{:S(2)}) %all-to-all-start.2) | async-done | bytes 262176 | tf_op jit(solution)/shard_map/all_to_all | solution.py:87
  29.3 3.1 all-to-all-start.1
  33.2 3.0 all-to-all-done.1
  36.1 3.4 all-to-all-start.3
  39.6 1.1 broadcast_multiply_fusion
  41.6 24.1 %scatter_fusion = f32[512,2,128]{2,1,0:T(2,128)} fusion(f32[512,2,128]{2,1,0:T(2,128)} %broadcast_in_dim.676, s32[256]{0:T(256)S(1)} %bitcast.254, f32[256,2,128]{2,1,0:T(2,128)S(1)} %broadcast_multiply_fusion), kind=kCustom, calls=%fused_computation.2 | custom fusion | bytes 787456 | tf_op jit(solution)/shard_map/scatter | solution.py:70
  67.0 4.0 all-to-all-start.4
  82.7 11.8 %select_add_fusion.2 = f32[128,128,72]{1,2,0:T(8,128)} fusion(f32[128,128]{1,0:T(8,128)S(1)} %bitcast.210, s32[128,128]{1,0:T(8,128)S(1)} %get-tuple-element.183, f32[128,128]{1,0:T(8,128)S(1)} %bitcast.211, s32[128,128]{1,0:T(8,128)S(1)} %get-tuple-element.179, f32[128,128]{1,0:T(8,128)S(1)} %bitcast.212, s32[128,128]{1,0:T(8,128)S(1)} %get-tuple-element.180, ...), kind=kLoop, calls=%fused_computation.119 | loop fusion | flops 27131904 | bytes 5767168 | tf_op jit(solution)/shard_map/add | solution.py:35
  94.6 11.6 %select_add_fusion = f32[128,128,72]{1,2,0:T(8,128)} fusion(f32[128,128]{1,0:T(8,128)S(1)} %bitcast.202, s32[128,128]{1,0:T(8,128)S(1)} %get-tuple-element.207, f32[128,128]{1,0:T(8,128)S(1)} %bitcast.203, s32[128,128]{1,0:T(8,128)S(1)} %get-tuple-element.203, f32[128,128]{1,0:T(8,128)S(1)} %bitcast.204, s32[128,128]{1,0:T(8,128)S(1)} %get-tuple-element.204, ...), kind=kLoop, calls=%fused_computation.51 | loop fusion | flops 27131904 | bytes 5767168 | tf_op jit(solution)/shard_map/add | solution.py:35
  106.2 11.7 %select_add_fusion.1 = f32[128,128,72]{1,2,0:T(8,128)} fusion(f32[128,128]{1,0:T(8,128)S(1)} %bitcast.186, s32[128,128]{1,0:T(8,128)S(1)} %get-tuple-element.195, f32[128,128]{1,0:T(8,128)S(1)} %bitcast.187, s32[128,128]{1,0:T(8,128)S(1)} %get-tuple-element.191, f32[128,128]{1,0:T(8,128)S(1)} %bitcast.188, s32[128,128]{1,0:T(8,128)S(1)} %get-tuple-element.192, ...), kind=kLoop, calls=%fused_computation.85 | loop fusion | flops 27131904 | bytes 5767168 | tf_op jit(solution)/shard_map/add | solution.py:35
  117.9 11.9 %select_add_fusion.3 = f32[128,128,72]{1,2,0:T(8,128)} fusion(f32[128,128]{1,0:T(8,128)S(1)} %bitcast.194, s32[128,128]{1,0:T(8,128)S(1)} %get-tuple-element.220, f32[128,128]{1,0:T(8,128)S(1)} %bitcast.195, s32[128,128]{1,0:T(8,128)S(1)} %get-tuple-element.224, f32[128,128]{1,0:T(8,128)S(1)} %bitcast.196, s32[128,128]{1,0:T(8,128)S(1)} %get-tuple-element.223, ...), kind=kLoop, calls=%fused_computation.153 | loop fusion | flops 27131904 | bytes 5767168 | tf_op jit(solution)/shard_map/add | solution.py:35
  130.6 3.5 all-to-all-start.5
  135.9 6.9 %all-to-all-done.5 = f32[8,4,16,2,128]{4,3,2,0,1:T(2,128)S(1)} async-done(((f32[8,4,16,2,128]{4,3,2,0,1:T(2,128)}), f32[8,4,16,2,128]{4,3,2,0,1:T(2,128)S(1)}, u32[]{:S(2)}, u32[]{:S(2)}) %all-to-all-start.5) | async-done | bytes 524320 | tf_op jit(solution)/shard_map/all_to_all | solution.py:79
  143.4 17.6 %fusion.12 = f32[128,2,72,72]{3,2,1,0:T(8,128)} fusion(f32[128,2,128]{2,1,0:T(2,128)S(1)} %copy.153, f32[128,128,72]{1,2,0:T(8,128)} %select_add_fusion.2, f32[128,128]{1,0:T(8,128)} %bitcast.234, s32[128,128]{1,0:T(8,128)S(1)} %get-tuple-element.177, f32[128,128]{1,0:T(8,128)} %bitcast.235, s32[128,128]{1,0:T(8,128)S(1)} %get-tuple-element.173, ...), kind=kOutput, calls=%fused_computation.18 | convolution fusion | flops 2067922944 | bytes 11206656 | tf_op jit(solution)/shard_map/bcru,brv->bcuv/dot_general | solution.py:121
  161.0 8.5 %copy.154 = f32[128,2,72,72]{0,3,2,1:T(8,128)} copy(f32[128,2,72,72]{3,2,1,0:T(8,128)} %fusion.12) | data formatting | bytes 10616832 | tf_op jit(solution)/shard_map/bcru,brv->bcuv/dot_general | solution.py:121
  169.5 17.6 %fusion.8 = f32[128,2,72,72]{3,2,1,0:T(8,128)} fusion(f32[128,2,128]{2,1,0:T(2,128)S(1)} %copy.159, f32[128,128,72]{1,2,0:T(8,128)} %select_add_fusion, f32[128,128]{1,0:T(8,128)S(1)} %bitcast.226, s32[128,128]{1,0:T(8,128)S(1)} %get-tuple-element.201, f32[128,128]{1,0:T(8,128)S(1)} %bitcast.227, s32[128,128]{1,0:T(8,128)S(1)} %get-tuple-element.197, ...), kind=kOutput, calls=%fused_computation.14 | convolution fusion | flops 2067922944 | bytes 11206656 | tf_op jit(solution)/shard_map/bcru,brv->bcuv/dot_general | solution.py:121
  187.2 8.5 %copy.160 = f32[128,2,72,72]{0,3,2,1:T(8,128)} copy(f32[128,2,72,72]{3,2,1,0:T(8,128)} %fusion.8) | data formatting | bytes 10616832 | tf_op jit(solution)/shard_map/bcru,brv->bcuv/dot_general | solution.py:121
  195.8 17.5 %fusion.10 = f32[128,2,72,72]{3,2,1,0:T(8,128)} fusion(f32[128,2,128]{2,1,0:T(2,128)S(1)} %copy.156, f32[128,128,72]{1,2,0:T(8,128)} %select_add_fusion.1, f32[128,128]{1,0:T(8,128)S(1)} %bitcast.242, s32[128,128]{1,0:T(8,128)S(1)} %get-tuple-element.214, f32[128,128]{1,0:T(8,128)S(1)} %bitcast.243, s32[128,128]{1,0:T(8,128)S(1)} %get-tuple-element.218, ...), kind=kOutput, calls=%fused_computation.16 | convolution fusion | flops 2067922944 | bytes 11206656 | tf_op jit(solution)/shard_map/bcru,brv->bcuv/dot_general | solution.py:121
  213.3 8.5 %copy.157 = f32[128,2,72,72]{0,3,2,1:T(8,128)} copy(f32[128,2,72,72]{3,2,1,0:T(8,128)} %fusion.10) | data formatting | bytes 10616832 | tf_op jit(solution)/shard_map/bcru,brv->bcuv/dot_general | solution.py:121
  221.9 17.5 %fusion.14 = f32[128,2,72,72]{3,2,1,0:T(8,128)} fusion(f32[128,2,128]{2,1,0:T(2,128)S(1)} %copy.150, f32[128,128,72]{1,2,0:T(8,128)} %select_add_fusion.3, f32[128,128]{1,0:T(8,128)S(1)} %bitcast.218, s32[128,128]{1,0:T(8,128)S(1)} %copy-done.8, f32[128,128]{1,0:T(8,128)S(1)} %bitcast.219, s32[128,128]{1,0:T(8,128)S(1)} %copy-done.4, ...), kind=kOutput, calls=%fused_computation.20 | convolution fusion | flops 2067922944 | bytes 11206656 | tf_op jit(solution)/shard_map/bcru,brv->bcuv/dot_general | solution.py:121
  239.4 8.4 %copy.151 = f32[128,2,72,72]{0,3,2,1:T(8,128)} copy(f32[128,2,72,72]{3,2,1,0:T(8,128)} %fusion.14) | data formatting | bytes 10616832 | tf_op jit(solution)/shard_map/bcru,brv->bcuv/dot_general | solution.py:121
  247.8 31.5 %fusion = f32[256,10368]{1,0:T(8,128)} fusion(f32[128,10368]{0,1:T(8,128)} %bitcast.177, f32[128,10368]{0,1:T(8,128)} %bitcast.178, f32[128,10368]{0,1:T(8,128)} %bitcast.176, f32[128,10368]{0,1:T(8,128)} %bitcast.179, s32[512]{0:T(512)S(1)} %eq.754), kind=kOutput, calls=%fused_computation.3 | convolution fusion | flops 16323641344 | bytes 31852544 | tf_op jit(solution)/shard_map/bs,bx->sx/dot_general | solution.py:125
  279.3 19.8 %reshape.426 = f32[16,16,2,72,72]{4,3,2,1,0:T(8,128)} reshape(f32[256,10368]{1,0:T(8,128)} %fusion) | data formatting | bytes 21233664 | tf_op jit(solution)/shard_map/reshape | solution.py:126
  299.1 10.8 %copy.180 = f32[16,16,2,72,72]{4,1,3,0,2:T(8,128)S(1)} copy(f32[16,16,2,72,72]{4,3,2,1,0:T(8,128)} %reshape.426) | data formatting | bytes 21233664 | tf_op jit(solution)/shard_map/reshape | solution.py:126
  309.9 10.1 %slice.506 = f32[2,16,72,16,8]{4,3,2,1,0:T(8,128)} slice(f32[2,16,72,16,72]{4,3,2,1,0:T(8,128)S(1)} %bitcast.171), slice={[0:2], [0:16], [0:72], [0:16], [64:72]} | slice | bytes 2359296 | tf_op jit(solution)/shard_map/slice | solution.py:47
  319.9 2.0 copy-done.2
  322.0 16.6 %reshape.427 = f32[2,16,72,1024]{3,2,1,0:T(8,128)} reshape(f32[2,16,72,16,64]{4,3,2,1,0:T(8,128)} %bitcast.172) | data formatting | bytes 18874368 | tf_op jit(solution)/shard_map/reshape | solution.py:45
  338.6 12.9 %pad.33 = f32[2,16,72,16,64]{4,3,2,1,0:T(8,128)} pad(f32[2,16,72,16,8]{4,3,2,1,0:T(8,128)} %slice.506, f32[]{:T(128)} %constant.251.clone.1), padding=0_0x0_0x0_0x0_0x0_56 | pad | bytes 10616836 | tf_op jit(solution)/shard_map/jit(_pad)/pad | solution.py:47
  351.5 16.7 %reshape.428 = f32[2,16,72,1024]{3,2,1,0:T(8,128)} reshape(f32[2,16,72,16,64]{4,3,2,1,0:T(8,128)} %pad.33) | data formatting | bytes 18874368 | tf_op jit(solution)/shard_map/reshape | solution.py:48
  368.1 13.1 %add_bitcast_fusion = f32[2,1032,16,72]{1,3,2,0:T(8,128)} fusion(f32[2,16,72,1024]{3,2,1,0:T(8,128)} %reshape.428, f32[2,16,72,1024]{3,2,1,0:T(8,128)} %reshape.427), kind=kLoop, calls=%fused_computation.12 | loop fusion | flops 2377728 | bytes 28385280 | tf_op jit(solution)/shard_map/transpose | solution.py:128
  381.2 8.3 %slice.507 = f32[2,1032,16,64]{1,3,2,0:T(8,128)} slice(f32[2,1032,16,72]{1,3,2,0:T(8,128)} %add_bitcast_fusion), slice={[0:2], [0:1032], [0:16], [0:64]} | slice | bytes 16908288 | tf_op jit(solution)/shard_map/slice | solution.py:45
  389.5 9.4 %copy.162 = f32[2,1032,1024]{2,1,0:T(8,128)} copy(f32[2,1032,1024]{1,2,0:T(8,128)} %bitcast.175) | data formatting | bytes 16908288 | tf_op jit(solution)/shard_map/reshape | solution.py:45
  398.9 4.8 %pad.36 = f32[2,1032,16,64]{1,3,2,0:T(8,128)} pad(f32[2,1032,16,8]{1,3,2,0:T(8,128)S(1)} %slice-done, f32[]{:T(128)} %constant.251.clone.1), padding=0_0x0_0x0_0x0_56 | pad | bytes 9510916 | tf_op jit(solution)/shard_map/jit(_pad)/pad | solution.py:47
  403.7 9.5 %copy.163 = f32[2,1032,1024]{2,1,0:T(8,128)} copy(f32[2,1032,1024]{1,2,0:T(8,128)} %bitcast.174) | data formatting | bytes 16908288 | tf_op jit(solution)/shard_map/reshape | solution.py:48
  413.1 12.1 %add_bitcast_fusion.1 = f32[2,1032,1032]{1,2,0:T(8,128)} fusion(f32[2,1032,1024]{2,1,0:T(8,128)} %copy.163, f32[2,1032,1024]{2,1,0:T(8,128)} %copy.162), kind=kLoop, calls=%fused_computation.13 | loop fusion | flops 2130048 | bytes 25428480 | tf_op jit(solution)/shard_map/transpose | solution.py:129
  425.3 1.3 slice.513
  428.4 3.8 collective-permute-start
  433.0 8.4 %slice.509 = f32[2,1024,1024]{1,2,0:T(8,128)} slice(f32[2,1032,1032]{1,2,0:T(8,128)} %add_bitcast_fusion.1), slice={[0:2], [0:1024], [0:1024]} | slice | bytes 16777216 | tf_op jit(solution)/shard_map/slice | solution.py:140
  442.3 1.5 fusion.208
  443.8 1.4 slice_add_fusion
  445.3 5.9 %scatter-add.11 = f32[1,1,2,1024,1024]{3,4,2,1,0:T(8,128)} dynamic-update-slice(f32[1,1,2,1024,1024]{3,4,2,1,0:T(8,128)} %bitcast.173, f32[1,1,2,8,1024]{3,4,2,1,0:T(8,128)S(1)} %bitcast.180, s32[]{:T(128)} %constant.247.clone.1, s32[]{:T(128)} %constant.247.clone.1, s32[]{:T(128)} %constant.247.clone.1, s32[]{:T(128)} %constant.247.clone.1, s32[]{:T(128)} %constant.247.clone.1) | dynamic-update-slice | bytes 131076 | tf_op jit(solution)/shard_map/scatter-add | solution.py:142
  451.2 2.6 scatter-add.14
  453.8 8.7 %copy.168 = f32[1,1,2,1024,1024]{4,3,2,1,0:T(8,128)} copy(f32[1,1,2,1024,1024]{3,4,2,1,0:T(8,128)} %scatter-add.14) | data formatting | bytes 16777216 | tf_op jit(solution)/shard_map/scatter-add | solution.py:143
  (104 shorter events, 24.2 us)
Async XLA Ops:
  0.0 72.0 %copy-start = (f32[16,8]{0,1:T(8,128)S(1)}, f32[16,8]{0,1:T(8,128)}, u32[]{:S(2)}) copy-start(f32[16,8]{0,1:T(8,128)} %param.19) | copy-start | bytes 1540
  3.9 13.8 %all-to-all-start = ((s32[8,4,16]{2,1,0:T(4,128)}), s32[8,4,16]{2,1,0:T(4,128)S(1)}, u32[]{:S(2)}, u32[]{:S(2)}) async-start(s32[8,4,16]{2,1,0:T(4,128)} %reshape.419), calls=%async_computation | async-start | bytes 32768 | tf_op jit(solution)/shard_map/all_to_all | solution.py:94
  17.7 11.6 %all-to-all-start.2 = ((s32[8,4,16,1,128]{4,2,1,3,0:T(8,128)}), s32[8,4,16,1,128]{4,2,1,3,0:T(8,128)S(1)}, u32[]{:S(2)}, u32[]{:S(2)}) async-start(s32[8,4,16,1,128]{4,2,1,3,0:T(8,128)} %bitcast.4), calls=%async_computation.2 | async-start | bytes 524288 | tf_op jit(solution)/shard_map/all_to_all | solution.py:87
  29.3 6.9 %all-to-all-start.1 = ((s32[4,1,128]{2,1,0:T(1,128)}), s32[4,1,128]{2,1,0:T(1,128)S(1)}, u32[]{:S(2)}, u32[]{:S(2)}) async-start(s32[4,1,128]{2,1,0:T(1,128)} %reshape.471), calls=%async_computation.1 | async-start | bytes 4096 | tf_op jit(solution)/shard_map/all_to_all | solution.py:93
  36.1 30.8 %all-to-all-start.3 = ((s32[8,4,16,1,128]{4,2,0,3,1:T(8,128)}), s32[8,4,16,1,128]{4,2,0,3,1:T(8,128)S(1)}, u32[]{:S(2)}, u32[]{:S(2)}) async-start(s32[8,4,16,1,128]{4,2,0,3,1:T(8,128)} %copy.146), calls=%async_computation.3 | async-start | bytes 524288 | tf_op jit(solution)/shard_map/all_to_all | solution.py:86
  67.0 62.8 %all-to-all-start.4 = ((f32[8,4,16,2,128]{4,3,2,1,0:T(2,128)}), f32[8,4,16,2,128]{4,3,2,1,0:T(2,128)S(1)}, u32[]{:S(2)}, u32[]{:S(2)}) async-start(f32[8,4,16,2,128]{4,3,2,1,0:T(2,128)} %bitcast.15), calls=%async_computation.4 | async-start | bytes 1048576 | tf_op jit(solution)/shard_map/all_to_all | solution.py:80
  130.6 12.3 %all-to-all-start.5 = ((f32[8,4,16,2,128]{4,3,2,0,1:T(2,128)}), f32[8,4,16,2,128]{4,3,2,0,1:T(2,128)S(1)}, u32[]{:S(2)}, u32[]{:S(2)}) async-start(f32[8,4,16,2,128]{4,3,2,0,1:T(2,128)} %copy.148), calls=%async_computation.5 | async-start | bytes 1048576 | tf_op jit(solution)/shard_map/all_to_all | solution.py:79
  161.0 8.5 %copy-start.19 = (s32[128,128]{1,0:T(8,128)S(1)}, s32[128,128]{1,0:T(8,128)}, u32[]{:S(2)}) copy-start(s32[128,128]{1,0:T(8,128)} %get-tuple-element.143) | copy-start | bytes 196612
  187.1 8.6 %copy-start.9 = (f32[128,128,1]{1,2,0:T(1,128)S(1)}, f32[128,128,1]{1,2,0:T(1,128)}, u32[]{:S(2)}) copy-start(f32[128,128,1]{1,2,0:T(1,128)} %get-tuple-element.105) | copy-start | bytes 196612
  187.1 8.6 %copy-start.10 = (f32[128,128,1]{1,2,0:T(1,128)S(1)}, f32[128,128,1]{1,2,0:T(1,128)}, u32[]{:S(2)}) copy-start(f32[128,128,1]{1,2,0:T(1,128)} %get-tuple-element.106) | copy-start | bytes 196612
  187.1 8.6 %copy-start.11 = (f32[128,128,1]{1,2,0:T(1,128)S(1)}, f32[128,128,1]{1,2,0:T(1,128)}, u32[]{:S(2)}) copy-start(f32[128,128,1]{1,2,0:T(1,128)} %get-tuple-element.107) | copy-start | bytes 196612
  187.1 8.6 %copy-start.12 = (f32[128,128,1]{1,2,0:T(1,128)S(1)}, f32[128,128,1]{1,2,0:T(1,128)}, u32[]{:S(2)}) copy-start(f32[128,128,1]{1,2,0:T(1,128)} %get-tuple-element.108) | copy-start | bytes 196612
  187.1 8.6 %copy-start.13 = (f32[128,128,1]{1,2,0:T(1,128)S(1)}, f32[128,128,1]{1,2,0:T(1,128)}, u32[]{:S(2)}) copy-start(f32[128,128,1]{1,2,0:T(1,128)} %get-tuple-element.109) | copy-start | bytes 196612
  187.2 8.6 %copy-start.14 = (f32[128,128,1]{1,2,0:T(1,128)S(1)}, f32[128,128,1]{1,2,0:T(1,128)}, u32[]{:S(2)}) copy-start(f32[128,128,1]{1,2,0:T(1,128)} %get-tuple-element.110) | copy-start | bytes 196612
  187.2 8.6 %copy-start.15 = (f32[128,128,1]{1,2,0:T(1,128)S(1)}, f32[128,128,1]{1,2,0:T(1,128)}, u32[]{:S(2)}) copy-start(f32[128,128,1]{1,2,0:T(1,128)} %get-tuple-element.111) | copy-start | bytes 196612
  187.2 8.6 %copy-start.16 = (f32[128,128,1]{1,2,0:T(1,128)S(1)}, f32[128,128,1]{1,2,0:T(1,128)}, u32[]{:S(2)}) copy-start(f32[128,128,1]{1,2,0:T(1,128)} %get-tuple-element.112) | copy-start | bytes 196612
  187.2 8.6 %copy-start.18 = (s32[128,128]{1,0:T(8,128)S(1)}, s32[128,128]{1,0:T(8,128)}, u32[]{:S(2)}) copy-start(s32[128,128]{1,0:T(8,128)} %get-tuple-element.137) | copy-start | bytes 196612
  213.3 8.5 %copy-start.3 = (s32[128,128]{1,0:T(8,128)S(1)}, s32[128,128]{1,0:T(8,128)}, u32[]{:S(2)}) copy-start(s32[128,128]{1,0:T(8,128)} %get-tuple-element.160) | copy-start | bytes 196612
  213.3 8.5 %copy-start.4 = (s32[128,128]{1,0:T(8,128)S(1)}, s32[128,128]{1,0:T(8,128)}, u32[]{:S(2)}) copy-start(s32[128,128]{1,0:T(8,128)} %get-tuple-element.161) | copy-start | bytes 196612
  213.3 8.5 %copy-start.5 = (s32[128,128]{1,0:T(8,128)S(1)}, s32[128,128]{1,0:T(8,128)}, u32[]{:S(2)}) copy-start(s32[128,128]{1,0:T(8,128)} %get-tuple-element.162) | copy-start | bytes 196612
  213.3 8.5 %copy-start.6 = (s32[128,128]{1,0:T(8,128)S(1)}, s32[128,128]{1,0:T(8,128)}, u32[]{:S(2)}) copy-start(s32[128,128]{1,0:T(8,128)} %get-tuple-element.163) | copy-start | bytes 196612
  213.3 8.5 %copy-start.7 = (s32[128,128]{1,0:T(8,128)S(1)}, s32[128,128]{1,0:T(8,128)}, u32[]{:S(2)}) copy-start(s32[128,128]{1,0:T(8,128)} %get-tuple-element.164) | copy-start | bytes 196612
  213.3 8.5 %copy-start.8 = (s32[128,128]{1,0:T(8,128)S(1)}, s32[128,128]{1,0:T(8,128)}, u32[]{:S(2)}) copy-start(s32[128,128]{1,0:T(8,128)} %get-tuple-element.165) | copy-start | bytes 196612
  213.3 8.5 %copy-start.17 = (s32[128,128]{1,0:T(8,128)S(1)}, s32[128,128]{1,0:T(8,128)}, u32[]{:S(2)}) copy-start(s32[128,128]{1,0:T(8,128)} %get-tuple-element.41) | copy-start | bytes 196612
  309.9 12.1 %copy-start.2 = (f32[16,16,2,72,72]{4,1,3,0,2:T(8,128)}, f32[16,16,2,72,72]{4,1,3,0,2:T(8,128)S(1)}, u32[]{:S(2)}) copy-start(f32[16,16,2,72,72]{4,1,3,0,2:T(8,128)S(1)} %copy.180) | copy-start | bytes 31850500
  389.5 9.4 %slice-start = ((f32[2,1032,16,72]{1,3,2,0:T(8,128)}), f32[2,1032,16,8]{1,3,2,0:T(8,128)S(1)}, s32[]{:S(2)}) async-start(f32[2,1032,16,72]{1,3,2,0:T(8,128)} %add_bitcast_fusion), calls=%async_computation.6 | async-start | bytes 2359296 | tf_op jit(solution)/shard_map/slice | solution.py:47
  426.9 15.1 %collective-permute-start.1 = (f32[2,8,1024]{2,1,0:T(8,128)S(1)}, f32[2,8,1024]{2,1,0:T(8,128)S(1)}, u32[]{:S(2)}, u32[]{:S(2)}) collective-permute-start(f32[2,8,1024]{2,1,0:T(8,128)S(1)} %copy.164), channel_id=1, source_target_pairs={} | collective-permute-start | bytes 196616 | tf_op jit(solution)/shard_map/ppermute | solution.py:19
  428.4 13.9 %collective-permute-start = (f32[2,8,1024]{2,1,0:T(8,128)S(1)}, f32[2,8,1024]{2,1,0:T(8,128)S(1)}, u32[]{:S(2)}, u32[]{:S(2)}) collective-permute-start(f32[2,8,1024]{2,1,0:T(8,128)S(1)} %slice_bitcast_fusion), channel_id=1, source_target_pairs={{0,4},{4,8},{8,12},{12,16},{16,20},{20,24},{24,28},{1,5},{5,9},{9,... | collective-permute-start | bytes 196616 | tf_op jit(solution)/shard_map/ppermute | solution.py:19
  441.3 9.8 %collective-permute-start.2 = (f32[2,8,8]{1,2,0:T(8,128)S(1)}, f32[2,8,8]{1,2,0:T(8,128)S(1)}, u32[]{:S(2)}, u32[]{:S(2)}) collective-permute-start(f32[2,8,8]{1,2,0:T(8,128)S(1)} %slice.515), channel_id=1, source_target_pairs={} | collective-permute-start | bytes 1544 | tf_op jit(solution)/shard_map/ppermute | solution.py:19
  451.2 11.3 %copy-start.1 = (f32[16,8]{0,1:T(8,128)S(1)}, f32[16,8]{0,1:T(8,128)}, u32[]{:S(2)}) copy-start(f32[16,8]{0,1:T(8,128)} %param.19) | copy-start | bytes 1540
where the time goes:
time: 469 us; the launch traced here: 463 us
  local copies, waits for them, and re-layouts  219 us (47%)
  matrix products  108 us (23%)
  other arithmetic  83.8 us (18%)
  starting transfers between devices  29.8 us (6%)
  waiting for transfers between devices  21.7 us (5%)
    dot_general x4, matrix products, shards(): jnp.einsum('bcru,brv->bcuv', weighted, rows_along_v, precision=highest)  70.2 us
    add x4, other arithmetic, spread_matrix(): matrix + jnp.where(places == first_cell[..., None] + tap_index, taps[...,...  47 us
    dot_general x4, local copies, waits for them, and re-layouts, shards(): jnp.einsum('bcru,brv->bcuv', weighted, rows_along_v, precision=highest)  33.9 us
    dot_general x1, matrix products, shards(): accum = jnp.einsum('bs,bx->sx', chosen, all_patches, precision=highest)  31.5 us
    reshape x2, local copies, waits for them, and re-layouts, shards(): accum.reshape(patches_across, patches_across, 2, extent, extent)  30.6 us
    reshape x2, local copies, waits for them, and re-layouts, unfold_edges(): edge_part = edge_part.reshape(leading + (block_count * SUB,))  26.1 us
    reshape x2, local copies, waits for them, and re-layouts, unfold_edges(): core_part = patches[..., :SUB].reshape(leading + (block_count * SUB,))  26 us
    scatter x2, local copies, waits for them, and re-layouts, bucket(): buffer = buffer.at[slot_index].set(values)  25.7 us
  transfers between devices with their start and end apart: 9, of which 4 were waited for; matrix products, arithmetic and copies ran while one was open for 24% of the time, Pallas kernels for 0%

commit v1 on v0

v1 whole, which is shorter than its diff:
```python
import functools

import jax
import jax.numpy as jnp
from jax import lax
from jax.experimental import pallas as pl
from jax.experimental.pallas import tpu as pltpu
from jax.sharding import PartitionSpec as P

TCOLS = 8
SUB = 64
KW = 8
OVER = 16
TILE = 1024
ROWS = 128
SIDE = TILE // SUB
PATCHES = SIDE * SIDE
ROW_BLOCK = 2 * (SUB + KW)
FIRST = SIDE
DUMMY = FIRST + PATCHES
UNROLL = 4

f32 = jnp.float32
bf16 = jnp.bfloat16


def lanes(shape):
    return lax.broadcasted_iota(jnp.int32, shape, len(shape) - 1)


def pack_kernel(peers, cap, routes, patch, vis, weight, cell, tap, out, count):
    blocks = vis.shape[0]
    lane = lanes((1, ROWS))

    def clear(d, carry):
        count[d] = 0
        out[d, 3 * cap] = jnp.zeros((1, ROWS), f32)
        return carry

    lax.fori_loop(0, peers, clear, 0)

    def place(b, carry):
        d = routes[b]
        k = count[d]
        count[d] = k + 1
        w = weight[pl.ds(b, 1), :]
        both = vis[b] * w
        c = cell[pl.ds(b, 1), :]
        t = tap[pl.ds(b, 1), :]
        at_u = ((t >> 4) << 3) | ((c >> 6) & 7)
        at_v = ((t & 15) << 3) | (c & 7)
        code = ((c >> 9) << 17) | (((c >> 3) & 7) << 14) | (at_u << 7) | at_v
        out[d, 3 * k] = both[0:1, :]
        out[d, 3 * k + 1] = both[1:2, :]
        out[d, 3 * k + 2] = code.astype(f32)
        row = out[d, 3 * cap]
        row = jnp.where(lane == k, patch[b].astype(f32), row)
        row = jnp.where(lane == cap, (k + 1).astype(f32), row)
        out[d, 3 * cap] = row
        return carry

    lax.fori_loop(0, blocks, place, 0, unroll=4)


def split(x):
    hi = x.astype(bf16)
    return hi, (x - hi.astype(f32)).astype(bf16)


def twice(x):
    return jnp.concatenate([x, x], axis=0)


def spread(groups, values):
    zero = jnp.zeros((16, ROWS), bf16)
    picks = [groups == 2.0 * g for g in range(SUB // 16)]
    return [[jnp.where(pick, value, zero) for pick in picks] for value in values]


def patch_product(re, im, code, table):
    sub = lax.broadcasted_iota(jnp.int32, (8, ROWS), 0)
    at_v = code & 127
    at_u = (code >> 7) & 127
    first_v = (code >> 14) & 7
    first_u = (code >> 17) & 7
    ku = jnp.take_along_axis(table, at_u, axis=1)
    kv = jnp.take_along_axis(table, at_v, axis=1)
    group_u = (first_u + jnp.where(sub < (at_u & 7), 1, 0)).astype(f32)
    group_v = (first_v + jnp.where(sub < (at_v & 7), 1, 0)).astype(f32)
    step_u = jnp.concatenate([group_u, group_u - 1.0], axis=0).astype(bf16)
    step_v = jnp.concatenate([group_v, group_v - 1.0], axis=0).astype(bf16)
    u_re, u_im = re * ku, im * ku
    zero = jnp.zeros((16, ROWS), bf16)

    re_hi, re_lo = split(twice(u_re))
    im_hi, im_lo = split(twice(u_im))
    last_hi, last_lo = split(jnp.concatenate([u_re, u_im], axis=0))
    re_hi, re_lo, im_hi, im_lo = spread(step_u, [re_hi, re_lo, im_hi, im_lo])
    past = twice(group_u).astype(bf16) == 8.0
    last_hi = jnp.where(past, last_hi, zero)
    last_lo = jnp.where(past, last_lo, zero)
    left_hi = jnp.concatenate(re_hi + im_hi + [last_hi], axis=0)
    left_lo = jnp.concatenate(re_lo + im_lo + [last_lo], axis=0)
    left = jnp.concatenate([left_hi, left_lo], axis=1)

    v_hi, v_lo = split(twice(kv))
    end = step_v == 8.0
    (hi_rows, lo_rows) = spread(step_v, [v_hi, v_lo])
    hi_rows.append(jnp.where(end, v_hi, zero))
    lo_rows.append(jnp.where(end, v_lo, zero))
    fill = [zero] * (8 - len(hi_rows))
    right = jnp.concatenate(hi_rows + fill + lo_rows + fill, axis=0)
    right = jnp.concatenate([right, right], axis=1)
    product = lax.dot_general(left, right, (((1,), (1,)), ((), ())), preferred_element_type=f32)
    return product[:, :ROWS] + product[:, ROWS:]


def tap_table(kernel):
    sub = lax.broadcasted_iota(jnp.int32, (8, ROWS), 0)
    lane = lanes((8, ROWS))
    which_tap = (sub - lane) & 7
    which_level = lane >> 3
    table = jnp.zeros((8, ROWS), f32)
    for a in range(KW):
        row = jnp.zeros((8, ROWS), f32)
        for o in range(OVER):
            row = jnp.where(which_level == o, kernel[o, a], row)
        table = jnp.where(which_tap == a, row, table)
    return table


def grid_kernel(peers, cap, with_low, kernel, arrived, out, right, *rest):
    low, rest = (rest[0], rest[1:]) if with_low else (None, rest)
    acc, stage, meta, slots, meta_sem, out_sems = rest
    meta_copy = pltpu.make_async_copy(arrived.at[:, 3 * cap, 0, :], meta, meta_sem)
    meta_copy.start()

    def clear(i, carry):
        acc[i] = jnp.zeros((ROW_BLOCK, ROWS), f32)
        return carry

    lax.fori_loop(0, DUMMY, clear, 0)
    table = tap_table(kernel)
    meta_copy.wait()

    def gather_source(s, total):
        for k in range(cap):
            slots[total + k] = (s * cap + k) * 512 + (meta[s, k].astype(jnp.int32) + FIRST)
        return total + meta[s, cap].astype(jnp.int32)

    total = lax.fori_loop(0, peers, gather_source, 0)
    for k in range(UNROLL):
        slots[total + k] = DUMMY

    def work(step, carry):
        for i in range(UNROLL):
            entry = slots[step * UNROLL + i]
            slot = entry >> 9
            where_to = entry & 511
            source = slot // cap
            k = slot - source * cap
            re = jnp.broadcast_to(arrived[source, 3 * k], (8, ROWS))
            im = jnp.broadcast_to(arrived[source, 3 * k + 1], (8, ROWS))
            code = jnp.broadcast_to(arrived[source, 3 * k + 2], (8, ROWS)).astype(jnp.int32)
            acc[where_to] += patch_product(re, im, code, table)
        return carry

    lax.fori_loop(0, (total + UNROLL - 1) // UNROLL, work, 0)

    lane = lanes((8, ROWS))

    def rows_of(c, h, band, col):
        part = acc[FIRST + band * SIDE + col, pl.ds(c * SUB + 8 * h, 8), :]
        if h == 0:
            part = part + acc[band * SIDE + col, pl.ds(2 * SUB + 8 * c, 8), :]
        return part

    def copy_out(band):
        rows = pl.ds(band * SUB, SUB)
        return pltpu.make_async_copy(stage.at[:, rows, :], out.at[:, rows, :], out_sems.at[band])

    def fold(pair, carry):
        for c in range(2):
            edge = jnp.zeros((8, ROWS), f32)
            for half in range(2):
                band = pair * 2 + half
                for h in range(8):
                    before = jnp.zeros((8, ROWS), f32)
                    for t in range(TILE // ROWS):
                        even = rows_of(c, h, band, 2 * t)
                        odd = rows_of(c, h, band, 2 * t + 1)
                        turned = pltpu.roll(odd, SUB, 1)
                        stage[c, pl.ds(band * SUB + 8 * h, 8), pl.ds(t * ROWS, ROWS)] = even + jnp.where(
                            lane < SUB, before, turned
                        )
                        before = turned
                    k = half * 8 + h
                    moved = pltpu.roll(before, 8 * k, 1) if k else before
                    edge = jnp.where((lane >> 3) == k, moved, edge)
            right[c, pair] = edge
        for half in range(2):
            copy_out(pair * 2 + half).start()
        return carry

    lax.fori_loop(0, SIDE // 2, fold, 0)
    if with_low:
        for c in range(2):
            before = jnp.zeros((8, ROWS), f32)
            for t in range(TILE // ROWS):
                rows = pl.ds(2 * SUB + 8 * c, 8)
                even = acc[FIRST + (SIDE - 1) * SIDE + 2 * t, rows, :]
                turned = pltpu.roll(acc[FIRST + (SIDE - 1) * SIDE + 2 * t + 1, rows, :], SUB, 1)
                low[c, :, pl.ds(t * ROWS, ROWS)] = even + jnp.where(lane < SUB, before, turned)
                before = turned
            low[c, :, pl.ds(TILE, ROWS)] = jnp.where(lane < KW, before, 0.0)

    def finish(band, carry):
        copy_out(band).wait()
        return carry

    lax.fori_loop(0, SIDE, finish, 0)


def edge_kernel(edge, grid_in, grid_out, columns, in_sems, out_sems):
    lane = lanes((8, ROWS))
    pairs = SIDE // 2

    def fetch(pair):
        rows = pl.ds(pair * 2 * SUB, 2 * SUB)
        return pltpu.make_async_copy(
            grid_in.at[:, rows, pl.ds(0, ROWS)], columns.at[:, rows, :], in_sems.at[pair]
        )

    def put(pair):
        rows = pl.ds(pair * 2 * SUB, 2 * SUB)
        return pltpu.make_async_copy(
            columns.at[:, rows, :], grid_out.at[:, rows, pl.ds(0, ROWS)], out_sems.at[pair]
        )

    for pair in range(pairs):
        fetch(pair).start()

    def add(pair, carry):
        fetch(pair).wait()
        for c in range(2):
            packed = edge[c, pair]
            for k in range(16):
                moved = pltpu.roll(packed, ROWS - 8 * k, 1) if k else packed
                rows = pl.ds(pair * 2 * SUB + 8 * k, 8)
                columns[c, rows, :] += jnp.where(lane < KW, moved, 0.0)
        put(pair).start()
        return carry

    lax.fori_loop(0, pairs, add, 0)
    for pair in range(pairs):
        put(pair).wait()


def shifted(block, axis, distance):
    devices = range(lax.axis_size(axis))
    route = [(i - distance, i) for i in devices if i - distance in devices]
    return lax.ppermute(block, axis, route)


def shards(visibilities, vis_weight, cell_index, tap_offsets, routes, patch_index, kernel):
    blocks = visibilities.shape[0]
    tile_count = lax.axis_size("tile")
    plane_count = lax.axis_size("wp")
    peers = tile_count * plane_count
    cap = max(2, 2 * blocks // peers)
    rows = 3 * cap + 1
    vmem = pl.BlockSpec(memory_space=pltpu.VMEM)
    smem = pl.BlockSpec(memory_space=pltpu.SMEM)
    hbm = pl.BlockSpec(memory_space=pl.ANY)

    buckets = pl.pallas_call(
        functools.partial(pack_kernel, peers, cap),
        out_shape=jax.ShapeDtypeStruct((peers, rows, 1, ROWS), f32),
        in_specs=[smem, smem, vmem, vmem, vmem, vmem],
        out_specs=vmem,
        scratch_shapes=[pltpu.SMEM((peers,), jnp.int32)],
        compiler_params=pltpu.CompilerParams(vmem_limit_bytes=16 << 20),
        name="pack",
    )(routes[:, 0], patch_index, visibilities, vis_weight, cell_index, tap_offsets)

    arrived = lax.all_to_all(buckets, ("tile", "wp"), split_axis=0, concat_axis=0, tiled=True)

    with_low = tile_count > TCOLS
    out_shape = [
        jax.ShapeDtypeStruct((2, TILE, TILE), f32),
        jax.ShapeDtypeStruct((2, SIDE // 2, 8, ROWS), f32),
    ]
    out_specs = [hbm, vmem]
    if with_low:
        out_shape.append(jax.ShapeDtypeStruct((2, KW, TILE + ROWS), f32))
        out_specs.append(vmem)
    results = pl.pallas_call(
        functools.partial(grid_kernel, peers, cap, with_low),
        out_shape=out_shape,
        in_specs=[smem, vmem],
        out_specs=out_specs,
        scratch_shapes=[
            pltpu.VMEM((DUMMY + 1, ROW_BLOCK, ROWS), f32),
            pltpu.VMEM((2, TILE, TILE), f32),
            pltpu.SMEM((peers, ROWS), f32),
            pltpu.SMEM((peers * cap + max(cap, UNROLL),), jnp.int32),
            pltpu.SemaphoreType.DMA,
            pltpu.SemaphoreType.DMA((SIDE,)),
        ],
        compiler_params=pltpu.CompilerParams(vmem_limit_bytes=48 << 20),
        name="grid",
    )(kernel, arrived)
    own, right = results[0], results[1]

    place = lax.axis_index("tile")
    from_left = shifted(right, "tile", 1)
    if with_low:
        from_left = jnp.where(place % TCOLS == 0, 0.0, from_left)
    own = pl.pallas_call(
        edge_kernel,
        out_shape=jax.ShapeDtypeStruct((2, TILE, TILE), f32),
        in_specs=[vmem, hbm],
        out_specs=hbm,
        scratch_shapes=[
            pltpu.VMEM((2, TILE, ROWS), f32),
            pltpu.SemaphoreType.DMA((SIDE // 2,)),
            pltpu.SemaphoreType.DMA((SIDE // 2,)),
        ],
        input_output_aliases={1: 0},
        compiler_params=pltpu.CompilerParams(vmem_limit_bytes=16 << 20),
        name="edges",
    )(from_left, own)
    if with_low:
        low = results[2]
        from_above = shifted(low, "tile", TCOLS)
        from_corner = shifted(low[:, :, TILE:], "tile", TCOLS + 1)
        from_corner = jnp.where(place % TCOLS == 0, 0.0, from_corner)
        own = own.at[:, :KW, :].add(from_above[:, :, :TILE])
        own = own.at[:, :KW, :ROWS].add(from_corner)
    return own.reshape(1, 1, 2, TILE, TILE)


def solution(mesh):
    in_specs = (
        P(("tile", "wp"), None, None),
        P(("tile", "wp"), None),
        P(("tile", "wp"), None),
        P(("tile", "wp"), None),
        P(("tile", "wp"), None),
        P(("tile", "wp")),
        P(),
    )
    out_specs = P("wp", "tile", None, None, None)
    return jax.shard_map(shards, mesh=mesh, in_specs=in_specs, out_specs=out_specs, check_vma=False)
```

time: 469 us -> 110 us (0.23)
  the two profiles are of different devices: /device:TPU:0 before, /device:TPU:13 now
where the time goes in v1:
time: 110 us; the launch traced here: 108 us
  Pallas kernels  70.6 us (64%)
  waiting for transfers between devices  23.2 us (21%)
  starting transfers between devices  8.36 us (8%)
  local copies, waits for them, and re-layouts  5.78 us (5%)
    pallas_call x1, Pallas kernels, shards(): pl.pallas_call(functools.partial(grid_kernel, peers, cap, with_low), out_...  64.6 us
    all_to_all x1, waiting for transfers between devices, shards(): lax.all_to_all(buckets, ('tile', 'wp'), split_axis=0, concat_axis=0, tile...  19.3 us
    all_to_all x1, starting transfers between devices, shards(): lax.all_to_all(buckets, ('tile', 'wp'), split_axis=0, concat_axis=0, tile...  6.3 us
    unnamed x13, local copies, waits for them, and re-layouts  5.78 us
    ppermute x1, waiting for transfers between devices, shifted(): return lax.ppermute(block, axis, route)  3.85 us
    pallas_call x1, Pallas kernels, shards(): pl.pallas_call(functools.partial(pack_kernel, peers, cap), out_shape=jax....  3.45 us
    pallas_call x1, Pallas kernels, shards(): pl.pallas_call(edge_kernel, out_shape=jax.ShapeDtypeStruct((2, TILE, TILE...  2.52 us
  transfers between devices with their start and end apart: 2, of which 2 were waited for; matrix products, arithmetic and copies ran while one was open for 1% of the time, Pallas kernels for 0%

profile of v1, /device:TPU:13, one launch (start us, length us, event | category | flops | bytes accessed | tf_op | source)
XLA Modules:
  0.0 107.9 jit_solution(4652591057951328204)
XLA Ops:
  0.0 0.0 copy-start
  0.0 0.9 copy-done
  1.0 0.0 copy-start.1
  1.0 0.9 copy-done.1
  1.9 0.0 copy-start.2
  1.9 0.9 copy-done.2
  2.8 0.0 copy-start.3
  2.8 0.9 copy-done.3
  3.7 0.0 copy-start.4
  3.7 0.7 copy-done.4
  4.3 0.0 copy-start.5
  4.3 0.7 copy-done.5
  5.0 3.4 %pack.1 = f32[32,49,1,128]{3,2,1,0:T(1,128)} custom-call(s32[256]{0:T(256)S(1)} %bitcast.2, s32[256]{0:T(256)S(1)} %copy-done.5, f32[256,2,128]{2,1,0:T(2,128)S(1)} %copy-done, f32[256,128]{1,0:T(8,128)S(1)} %copy-done.1, s32[256,128]{1,0:T(8,128)S(1)} %copy-done.2, s32[256,128]{1,0:T(8,128)S(1)} %copy-done.3), custom_call_target="tpu_custom_call" | custom-call | tf_op jit(solution)/shard_map/pack/pallas_call | solution.py:276
  8.5 6.3 %all-to-all-start = ((f32[32,49,1,128]{3,2,1,0:T(1,128)}), f32[32,49,1,128]{3,2,1,0:T(1,128)S(1)}, u32[]{:S(2)}, u32[]{:S(2)}) async-start(f32[32,49,1,128]{3,2,1,0:T(1,128)} %pack.1), calls=%async_computation | async-start | bytes 1605632 | tf_op jit(solution)/shard_map/all_to_all | solution.py:286
  14.8 0.8 copy.9.kernel
  15.5 19.3 %all-to-all-done.arrived = f32[32,49,1,128]{3,2,1,0:T(1,128)S(1)} async-done(((f32[32,49,1,128]{3,2,1,0:T(1,128)}), f32[32,49,1,128]{3,2,1,0:T(1,128)S(1)}, u32[]{:S(2)}, u32[]{:S(2)}) %all-to-all-start) | async-done | bytes 802848 | tf_op jit(solution)/shard_map/all_to_all | solution.py:286
  34.9 64.6 %grid.1 = (f32[2,1024,1024]{2,1,0:T(8,128)}, f32[2,8,8,128]{3,2,1,0:T(8,128)S(1)}) custom-call(f32[16,8]{1,0:T(8,128)S(1)} %copy.9.kernel, f32[32,49,1,128]{3,2,1,0:T(1,128)S(1)} %all-to-all-done.arrived), custom_call_target="tpu_custom_call" | custom-call | tf_op jit(solution)/shard_map/grid/pallas_call | solution.py:297
  99.5 2.1 %collective-permute-start = (f32[2,8,8,128]{3,2,1,0:T(8,128)S(1)}, f32[2,8,8,128]{3,2,1,0:T(8,128)S(1)}, u32[]{:S(2)}, u32[]{:S(2)}) collective-permute-start(f32[2,8,8,128]{3,2,1,0:T(8,128)S(1)} %get-tuple-element.7), channel_id=1, source_target_pairs={{0,4},{4,8},{8,12},{12,16},{16,20},{20,24},{24,28},{1,5},{5,9},{9,... | collective-permute-start | bytes 196616 | tf_op jit(solution)/shard_map/ppermute | solution.py:262
  101.5 3.8 %collective-permute-done.edge = f32[2,8,8,128]{3,2,1,0:T(8,128)S(1)} collective-permute-done((f32[2,8,8,128]{3,2,1,0:T(8,128)S(1)}, f32[2,8,8,128]{3,2,1,0:T(8,128)S(1)}, u32[]{:S(2)}, u32[]{:S(2)}) %collective-permute-start) | collective-permute-done | bytes 65568 | tf_op jit(solution)/shard_map/ppermute | solution.py:262
  105.4 2.5 %edges.1 = f32[2,1024,1024]{2,1,0:T(8,128)} custom-call(f32[2,8,8,128]{3,2,1,0:T(8,128)S(1)} %collective-permute-done.edge, f32[2,1024,1024]{2,1,0:T(8,128)} %get-tuple-element.8.grid_in), custom_call_target="tpu_custom_call", output_to_operand_aliasing={{}: (1, {})} | custom-call | tf_op jit(solution)/shard_map/edges/pallas_call | solution.py:319
Async XLA Ops:
  0.0 0.9 copy-start
  1.0 0.9 copy-start.1
  1.9 0.9 copy-start.2
  2.8 0.9 copy-start.3
  3.7 0.7 copy-start.4
  4.3 0.7 copy-start.5
  8.5 26.4 %all-to-all-start = ((f32[32,49,1,128]{3,2,1,0:T(1,128)}), f32[32,49,1,128]{3,2,1,0:T(1,128)S(1)}, u32[]{:S(2)}, u32[]{:S(2)}) async-start(f32[32,49,1,128]{3,2,1,0:T(1,128)} %pack.1), calls=%async_computation | async-start | bytes 1605632 | tf_op jit(solution)/shard_map/all_to_all | solution.py:286
  99.5 5.9 %collective-permute-start = (f32[2,8,8,128]{3,2,1,0:T(8,128)S(1)}, f32[2,8,8,128]{3,2,1,0:T(8,128)S(1)}, u32[]{:S(2)}, u32[]{:S(2)}) collective-permute-start(f32[2,8,8,128]{3,2,1,0:T(8,128)S(1)} %get-tuple-element.7), channel_id=1, source_target_pairs={{0,4},{4,8},{8,12},{12,16},{16,20},{20,24},{24,28},{1,5},{5,9},{9,... | collective-permute-start | bytes 196616 | tf_op jit(solution)/shard_map/ppermute | solution.py:262

commit v2 on v1

--- a/solution.py
+++ b/solution.py
@@ -18,7 +18,7 @@
 ROW_BLOCK = 2 * (SUB + KW)
 FIRST = SIDE
 DUMMY = FIRST + PATCHES
-UNROLL = 4
+UNROLL = 8
 
 f32 = jnp.float32
 bf16 = jnp.bfloat16
@@ -28,38 +28,63 @@
     return lax.broadcasted_iota(jnp.int32, shape, len(shape) - 1)
 
 
-def pack_kernel(peers, cap, routes, patch, vis, weight, cell, tap, out, count):
+def pack_kernel(peers, cap, routes, patch, vis, weight, cell, tap, out, *scratch):
+    routes_s, patch_s, vis_v, weight_v, cell_v, tap_v, meta, meta_v, place, sems = scratch
     blocks = vis.shape[0]
-    lane = lanes((1, ROWS))
+    rows = 3 * cap + 1
+    sources = (routes, patch, vis, weight, cell, tap)
+    targets = (routes_s, patch_s, vis_v, weight_v, cell_v, tap_v)
+    copies = [pltpu.make_async_copy(a, b, sems.at[i]) for i, (a, b) in enumerate(zip(sources, targets))]
+    for copy in copies:
+        copy.start()
 
     def clear(d, carry):
-        count[d] = 0
-        out[d, 3 * cap] = jnp.zeros((1, ROWS), f32)
-        return carry
-
-    lax.fori_loop(0, peers, clear, 0)
-
-    def place(b, carry):
-        d = routes[b]
-        k = count[d]
-        count[d] = k + 1
-        w = weight[pl.ds(b, 1), :]
-        both = vis[b] * w
-        c = cell[pl.ds(b, 1), :]
-        t = tap[pl.ds(b, 1), :]
+        meta[d, cap] = 0
+        return carry
+
+    lax.fori_loop(0, peers, clear, 0, unroll=8)
+    copies[0].wait()
+    copies[1].wait()
+
+    def choose(b, carry):
+        d = routes_s[b]
+        k = meta[d, cap]
+        meta[d, cap] = k + 1
+        meta[d, k] = patch_s[b]
+        place[b] = d * rows + 3 * k
+        return carry
+
+    lax.fori_loop(0, blocks, choose, 0, unroll=8)
+    meta_copy = pltpu.make_async_copy(meta, meta_v, sems.at[6])
+    meta_copy.start()
+    for copy in copies[2:]:
+        copy.wait()
+
+    def move(step, carry):
+        first = pl.multiple_of(step * 8, 8)
+        block_rows = pl.ds(first, 8)
+        w = weight_v[block_rows, :]
+        c = cell_v[block_rows, :]
+        t = tap_v[block_rows, :]
         at_u = ((t >> 4) << 3) | ((c >> 6) & 7)
         at_v = ((t & 15) << 3) | (c & 7)
-        code = ((c >> 9) << 17) | (((c >> 3) & 7) << 14) | (at_u << 7) | at_v
-        out[d, 3 * k] = both[0:1, :]
-        out[d, 3 * k + 1] = both[1:2, :]
-        out[d, 3 * k + 2] = code.astype(f32)
-        row = out[d, 3 * cap]
-        row = jnp.where(lane == k, patch[b].astype(f32), row)
-        row = jnp.where(lane == cap, (k + 1).astype(f32), row)
-        out[d, 3 * cap] = row
-        return carry
-
-    lax.fori_loop(0, blocks, place, 0, unroll=4)
+        code = (((c >> 9) << 17) | (((c >> 3) & 7) << 14) | (at_u << 7) | at_v).astype(f32)
+        for i in range(8):
+            row = place[first + i]
+            both = vis_v[first + i] * w[i : i + 1, :]
+            out[row] = both[0:1, :]
+            out[row + 1] = both[1:2, :]
+            out[row + 2] = code[i : i + 1, :]
+        return carry
+
+    lax.fori_loop(0, blocks // 8, move, 0)
+    meta_copy.wait()
+
+    def put_meta(d, carry):
+        out[d * rows + 3 * cap] = meta_v[pl.ds(d, 1), :].astype(f32)
+        return carry
+
+    lax.fori_loop(0, peers, put_meta, 0, unroll=8)
 
 
 def split(x):
@@ -71,32 +96,30 @@
     return jnp.concatenate([x, x], axis=0)
 
 
-def spread(groups, values):
+def spread(groups, count, values):
     zero = jnp.zeros((16, ROWS), bf16)
-    picks = [groups == 2.0 * g for g in range(SUB // 16)]
+    picks = [groups == 2.0 * g for g in range(count)]
     return [[jnp.where(pick, value, zero) for pick in picks] for value in values]
 
 
-def patch_product(re, im, code, table):
+def patch_product(re, im, code, parity, table):
     sub = lax.broadcasted_iota(jnp.int32, (8, ROWS), 0)
     at_v = code & 127
     at_u = (code >> 7) & 127
-    first_v = (code >> 14) & 7
-    first_u = (code >> 17) & 7
     ku = jnp.take_along_axis(table, at_u, axis=1)
     kv = jnp.take_along_axis(table, at_v, axis=1)
-    group_u = (first_u + jnp.where(sub < (at_u & 7), 1, 0)).astype(f32)
-    group_v = (first_v + jnp.where(sub < (at_v & 7), 1, 0)).astype(f32)
-    step_u = jnp.concatenate([group_u, group_u - 1.0], axis=0).astype(bf16)
-    step_v = jnp.concatenate([group_v, group_v - 1.0], axis=0).astype(bf16)
+    group_u = ((code >> 17) & 7) + jnp.where(sub < (at_u & 7), 1, 0)
+    group_v = ((code >> 14) & 7) + jnp.where(sub < (at_v & 7), 1, 0) + 8 * parity
+    step_u = jnp.concatenate([group_u, group_u - 1], axis=0).astype(f32).astype(bf16)
+    step_v = jnp.concatenate([group_v & 15, (group_v + 15) & 15], axis=0).astype(f32).astype(bf16)
     u_re, u_im = re * ku, im * ku
     zero = jnp.zeros((16, ROWS), bf16)
 
     re_hi, re_lo = split(twice(u_re))
     im_hi, im_lo = split(twice(u_im))
     last_hi, last_lo = split(jnp.concatenate([u_re, u_im], axis=0))
-    re_hi, re_lo, im_hi, im_lo = spread(step_u, [re_hi, re_lo, im_hi, im_lo])
-    past = twice(group_u).astype(bf16) == 8.0
+    re_hi, re_lo, im_hi, im_lo = spread(step_u, SUB // 16, [re_hi, re_lo, im_hi, im_lo])
+    past = twice(group_u).astype(f32).astype(bf16) == 8.0
     last_hi = jnp.where(past, last_hi, zero)
     last_lo = jnp.where(past, last_lo, zero)
     left_hi = jnp.concatenate(re_hi + im_hi + [last_hi], axis=0)
@@ -104,12 +127,8 @@
     left = jnp.concatenate([left_hi, left_lo], axis=1)
 
     v_hi, v_lo = split(twice(kv))
-    end = step_v == 8.0
-    (hi_rows, lo_rows) = spread(step_v, [v_hi, v_lo])
-    hi_rows.append(jnp.where(end, v_hi, zero))
-    lo_rows.append(jnp.where(end, v_lo, zero))
-    fill = [zero] * (8 - len(hi_rows))
-    right = jnp.concatenate(hi_rows + fill + lo_rows + fill, axis=0)
+    hi_rows, lo_rows = spread(step_v, ROWS // 16, [v_hi, v_lo])
+    right = jnp.concatenate(hi_rows + lo_rows, axis=0)
     right = jnp.concatenate([right, right], axis=1)
     product = lax.dot_general(left, right, (((1,), (1,)), ((), ())), preferred_element_type=f32)
     return product[:, :ROWS] + product[:, ROWS:]
@@ -124,45 +143,50 @@
     for a in range(KW):
         row = jnp.zeros((8, ROWS), f32)
         for o in range(OVER):
-            row = jnp.where(which_level == o, kernel[o, a], row)
+            row = jnp.where(which_level == o, kernel[a, o], row)
         table = jnp.where(which_tap == a, row, table)
     return table
 
 
 def grid_kernel(peers, cap, with_low, kernel, arrived, out, right, *rest):
     low, rest = (rest[0], rest[1:]) if with_low else (None, rest)
-    acc, stage, meta, slots, meta_sem, out_sems = rest
-    meta_copy = pltpu.make_async_copy(arrived.at[:, 3 * cap, 0, :], meta, meta_sem)
+    acc, stage, meta_v, meta, slots, meta_sem, out_sems = rest
+    rows = 3 * cap + 1
+    lane_row = lanes((1, ROWS))
+
+    def entries(s, carry):
+        row = arrived[s * rows + 3 * cap].astype(jnp.int32)
+        entry = (s * rows + 3 * lane_row) * 512 + (row + FIRST)
+        meta_v[pl.ds(s, 1), :] = jnp.where(lane_row < cap, entry, row)
+        return carry
+
+    lax.fori_loop(0, peers, entries, 0, unroll=8)
+    meta_copy = pltpu.make_async_copy(meta_v, meta, meta_sem)
     meta_copy.start()
-
-    def clear(i, carry):
-        acc[i] = jnp.zeros((ROW_BLOCK, ROWS), f32)
-        return carry
-
-    lax.fori_loop(0, DUMMY, clear, 0)
     table = tap_table(kernel)
     meta_copy.wait()
-
-    def gather_source(s, total):
+    share = (DUMMY + peers - 1) // peers
+
+    def prepare(s, total):
         for k in range(cap):
-            slots[total + k] = (s * cap + k) * 512 + (meta[s, k].astype(jnp.int32) + FIRST)
-        return total + meta[s, cap].astype(jnp.int32)
-
-    total = lax.fori_loop(0, peers, gather_source, 0)
+            slots[total + k] = meta[s, k]
+        for i in range(share):
+            acc[s * share + i] = jnp.zeros((ROW_BLOCK, ROWS), f32)
+        return total + meta[s, cap]
+
+    total = lax.fori_loop(0, peers, prepare, 0)
     for k in range(UNROLL):
         slots[total + k] = DUMMY
 
     def work(step, carry):
         for i in range(UNROLL):
             entry = slots[step * UNROLL + i]
-            slot = entry >> 9
+            row = entry >> 9
             where_to = entry & 511
-            source = slot // cap
-            k = slot - source * cap
-            re = jnp.broadcast_to(arrived[source, 3 * k], (8, ROWS))
-            im = jnp.broadcast_to(arrived[source, 3 * k + 1], (8, ROWS))
-            code = jnp.broadcast_to(arrived[source, 3 * k + 2], (8, ROWS)).astype(jnp.int32)
-            acc[where_to] += patch_product(re, im, code, table)
+            re = jnp.broadcast_to(arrived[row], (8, ROWS))
+            im = jnp.broadcast_to(arrived[row + 1], (8, ROWS))
+            code = jnp.broadcast_to(arrived[row + 2], (8, ROWS)).astype(jnp.int32)
+            acc[where_to] += patch_product(re, im, code, entry & 1, table)
         return carry
 
     lax.fori_loop(0, (total + UNROLL - 1) // UNROLL, work, 0)
@@ -189,11 +213,10 @@
                     for t in range(TILE // ROWS):
                         even = rows_of(c, h, band, 2 * t)
                         odd = rows_of(c, h, band, 2 * t + 1)
-                        turned = pltpu.roll(odd, SUB, 1)
                         stage[c, pl.ds(band * SUB + 8 * h, 8), pl.ds(t * ROWS, ROWS)] = even + jnp.where(
-                            lane < SUB, before, turned
+                            lane < SUB, before, odd
                         )
-                        before = turned
+                        before = odd
                     k = half * 8 + h
                     moved = pltpu.roll(before, 8 * k, 1) if k else before
                     edge = jnp.where((lane >> 3) == k, moved, edge)
@@ -209,9 +232,9 @@
             for t in range(TILE // ROWS):
                 rows = pl.ds(2 * SUB + 8 * c, 8)
                 even = acc[FIRST + (SIDE - 1) * SIDE + 2 * t, rows, :]
-                turned = pltpu.roll(acc[FIRST + (SIDE - 1) * SIDE + 2 * t + 1, rows, :], SUB, 1)
-                low[c, :, pl.ds(t * ROWS, ROWS)] = even + jnp.where(lane < SUB, before, turned)
-                before = turned
+                odd = acc[FIRST + (SIDE - 1) * SIDE + 2 * t + 1, rows, :]
+                low[c, :, pl.ds(t * ROWS, ROWS)] = even + jnp.where(lane < SUB, before, odd)
+                before = odd
             low[c, :, pl.ds(TILE, ROWS)] = jnp.where(lane < KW, before, 0.0)
 
     def finish(band, carry):
@@ -275,11 +298,22 @@
 
     buckets = pl.pallas_call(
         functools.partial(pack_kernel, peers, cap),
-        out_shape=jax.ShapeDtypeStruct((peers, rows, 1, ROWS), f32),
-        in_specs=[smem, smem, vmem, vmem, vmem, vmem],
+        out_shape=jax.ShapeDtypeStruct((peers * rows, 1, ROWS), f32),
+        in_specs=[hbm] * 6,
         out_specs=vmem,
-        scratch_shapes=[pltpu.SMEM((peers,), jnp.int32)],
-        compiler_params=pltpu.CompilerParams(vmem_limit_bytes=16 << 20),
+        scratch_shapes=[
+            pltpu.SMEM((blocks,), jnp.int32),
+            pltpu.SMEM((blocks,), jnp.int32),
+            pltpu.VMEM((blocks, 2, ROWS), f32),
+            pltpu.VMEM((blocks, ROWS), f32),
+            pltpu.VMEM((blocks, ROWS), jnp.int32),
+            pltpu.VMEM((blocks, ROWS), jnp.int32),
+            pltpu.SMEM((peers, ROWS), jnp.int32),
+            pltpu.VMEM((peers, ROWS), jnp.int32),
+            pltpu.SMEM((blocks,), jnp.int32),
+            pltpu.SemaphoreType.DMA((7,)),
+        ],
+        compiler_params=pltpu.CompilerParams(vmem_limit_bytes=60 << 20),
         name="pack",
     )(routes[:, 0], patch_index, visibilities, vis_weight, cell_index, tap_offsets)
 
@@ -300,16 +334,17 @@
         in_specs=[smem, vmem],
         out_specs=out_specs,
         scratch_shapes=[
-            pltpu.VMEM((DUMMY + 1, ROW_BLOCK, ROWS), f32),
+            pltpu.VMEM((-(-DUMMY // peers) * peers + 1, ROW_BLOCK, ROWS), f32),
             pltpu.VMEM((2, TILE, TILE), f32),
-            pltpu.SMEM((peers, ROWS), f32),
+            pltpu.VMEM((peers, ROWS), jnp.int32),
+            pltpu.SMEM((peers, ROWS), jnp.int32),
             pltpu.SMEM((peers * cap + max(cap, UNROLL),), jnp.int32),
             pltpu.SemaphoreType.DMA,
             pltpu.SemaphoreType.DMA((SIDE,)),
         ],
         compiler_params=pltpu.CompilerParams(vmem_limit_bytes=48 << 20),
         name="grid",
-    )(kernel, arrived)
+    )(kernel.T, arrived)
     own, right = results[0], results[1]
 
     place = lax.axis_index("tile")

time: 110 us -> 82.9 us (0.75)
  the two profiles are of different devices: /device:TPU:13 before, /device:TPU:12 now
where the time goes in v2:
time: 82.9 us; the launch traced here: 84.1 us
  Pallas kernels  50.6 us (61%)
  blocking collectives  25.7 us (31%)
  waiting for transfers between devices  5.13 us (6%)
  starting transfers between devices  1.92 us (2%)
    pallas_call x1, Pallas kernels, shards(): pl.pallas_call(functools.partial(grid_kernel, peers, cap, with_low), out_...  43.6 us
    all_to_all x1, blocking collectives, shards(): lax.all_to_all(buckets, ('tile', 'wp'), split_axis=0, concat_axis=0, tile...  25.7 us
    ppermute x1, waiting for transfers between devices, shifted(): return lax.ppermute(block, axis, route)  5.13 us
    pallas_call x1, Pallas kernels, shards(): pl.pallas_call(functools.partial(pack_kernel, peers, cap), out_shape=jax....  4.49 us
    pallas_call x1, Pallas kernels, shards(): pl.pallas_call(edge_kernel, out_shape=jax.ShapeDtypeStruct((2, TILE, TILE...  2.52 us
    ppermute x1, starting transfers between devices, shifted(): return lax.ppermute(block, axis, route)  1.92 us
  transfers between devices with their start and end apart: 1, of which 1 were waited for; matrix products, arithmetic and copies ran while one was open for 0% of the time, Pallas kernels for 0%

profile of v2, /device:TPU:12, one launch (start us, length us, event | category | flops | bytes accessed | tf_op | source)
XLA Modules:
  0.0 84.1 jit_solution(16571219813119315129)
XLA Ops:
  0.0 4.5 %pack.1 = f32[1568,1,128]{2,1,0:T(1,128)} custom-call(s32[256]{0:T(256)} %bitcast.4, s32[256]{0:T(256)} %patch.1, f32[256,2,128]{2,1,0:T(2,128)} %vis.1, f32[256,128]{1,0:T(8,128)} %weight.1, s32[256,128]{1,0:T(8,128)} %cell.1, s32[256,128]{1,0:T(8,128)} %tap.1), custom_call_target="tpu_custom_call" | custom-call | tf_op jit(solution)/shard_map/pack/pallas_call | solution.py:299
  4.5 25.7 %all_to_all.5.arrived = f32[1568,1,128]{2,1,0:T(1,128)S(1)} all-to-all(f32[1568,1,128]{2,1,0:T(1,128)} %pack.1), channel_id=1, replica_groups=mesh['tile'=8,'wp'=4] {'tile','wp'}, dimensions={0} | all-to-all | bytes 1605632 | tf_op jit(solution)/shard_map/all_to_all | solution.py:320
  30.2 0.0 copy-start
  30.2 0.7 copy-done
  30.9 43.6 %grid.1 = (f32[2,1024,1024]{2,1,0:T(8,128)}, f32[2,8,8,128]{3,2,1,0:T(8,128)S(1)}) custom-call(f32[8,16]{1,0:T(8,128)S(1)} %bitcast.3, f32[1568,1,128]{2,1,0:T(1,128)S(1)} %all_to_all.5.arrived), custom_call_target="tpu_custom_call" | custom-call | tf_op jit(solution)/shard_map/grid/pallas_call | solution.py:331
  74.5 1.9 %collective-permute-start = (f32[2,8,8,128]{3,2,1,0:T(8,128)S(1)}, f32[2,8,8,128]{3,2,1,0:T(8,128)S(1)}, u32[]{:S(2)}, u32[]{:S(2)}) collective-permute-start(f32[2,8,8,128]{3,2,1,0:T(8,128)S(1)} %get-tuple-element.7), channel_id=1, source_target_pairs={{0,4},{4,8},{8,12},{12,16},{16,20},{20,24},{24,28},{1,5},{5,9},{9,... | collective-permute-start | bytes 196616 | tf_op jit(solution)/shard_map/ppermute | solution.py:285
  76.4 5.1 %collective-permute-done.edge = f32[2,8,8,128]{3,2,1,0:T(8,128)S(1)} collective-permute-done((f32[2,8,8,128]{3,2,1,0:T(8,128)S(1)}, f32[2,8,8,128]{3,2,1,0:T(8,128)S(1)}, u32[]{:S(2)}, u32[]{:S(2)}) %collective-permute-start) | collective-permute-done | bytes 65568 | tf_op jit(solution)/shard_map/ppermute | solution.py:285
  81.5 2.5 %edges.1 = f32[2,1024,1024]{2,1,0:T(8,128)} custom-call(f32[2,8,8,128]{3,2,1,0:T(8,128)S(1)} %collective-permute-done.edge, f32[2,1024,1024]{2,1,0:T(8,128)} %get-tuple-element.8.grid_in), custom_call_target="tpu_custom_call", output_to_operand_aliasing={{}: (1, {})} | custom-call | tf_op jit(solution)/shard_map/edges/pallas_call | solution.py:354
Async XLA Ops:
  30.2 0.7 copy-start
  74.5 7.1 %collective-permute-start = (f32[2,8,8,128]{3,2,1,0:T(8,128)S(1)}, f32[2,8,8,128]{3,2,1,0:T(8,128)S(1)}, u32[]{:S(2)}, u32[]{:S(2)}) collective-permute-start(f32[2,8,8,128]{3,2,1,0:T(8,128)S(1)} %get-tuple-element.7), channel_id=1, source_target_pairs={{0,4},{4,8},{8,12},{12,16},{16,20},{20,24},{24,28},{1,5},{5,9},{9,... | collective-permute-start | bytes 196616 | tf_op jit(solution)/shard_map/ppermute | solution.py:285

commit v3 on v2

--- a/solution.py
+++ b/solution.py
@@ -18,7 +18,7 @@
 ROW_BLOCK = 2 * (SUB + KW)
 FIRST = SIDE
 DUMMY = FIRST + PATCHES
-UNROLL = 8
+UNROLL = 16
 
 f32 = jnp.float32
 bf16 = jnp.bfloat16

time: 82.9 us -> 76.5 us (0.923)
  the two profiles are of different devices: /device:TPU:12 before, /device:TPU:9 now
where the time goes in v3:
time: 76.5 us; the launch traced here: 76.2 us
  Pallas kernels  42.4 us (55%)
  blocking collectives  26.8 us (35%)
  waiting for transfers between devices  4.35 us (6%)
  starting transfers between devices  1.92 us (3%)
    pallas_call x1, Pallas kernels, shards(): pl.pallas_call(functools.partial(grid_kernel, peers, cap, with_low), out_...  35.4 us
    all_to_all x1, blocking collectives, shards(): lax.all_to_all(buckets, ('tile', 'wp'), split_axis=0, concat_axis=0, tile...  26.8 us
    pallas_call x1, Pallas kernels, shards(): pl.pallas_call(functools.partial(pack_kernel, peers, cap), out_shape=jax....  4.49 us
    ppermute x1, waiting for transfers between devices, shifted(): return lax.ppermute(block, axis, route)  4.35 us
    pallas_call x1, Pallas kernels, shards(): pl.pallas_call(edge_kernel, out_shape=jax.ShapeDtypeStruct((2, TILE, TILE...  2.52 us
    ppermute x1, starting transfers between devices, shifted(): return lax.ppermute(block, axis, route)  1.92 us
  transfers between devices with their start and end apart: 1, of which 1 were waited for; matrix products, arithmetic and copies ran while one was open for 0% of the time, Pallas kernels for 0%

profile of v3, /device:TPU:9, one launch (start us, length us, event | category | flops | bytes accessed | tf_op | source)
XLA Modules:
  0.0 76.2 jit_solution(13870177665950968578)
XLA Ops:
  0.0 4.5 %pack.1 = f32[1568,1,128]{2,1,0:T(1,128)} custom-call(s32[256]{0:T(256)} %bitcast.4, s32[256]{0:T(256)} %patch.1, f32[256,2,128]{2,1,0:T(2,128)} %vis.1, f32[256,128]{1,0:T(8,128)} %weight.1, s32[256,128]{1,0:T(8,128)} %cell.1, s32[256,128]{1,0:T(8,128)} %tap.1), custom_call_target="tpu_custom_call" | custom-call | tf_op jit(solution)/shard_map/pack/pallas_call | solution.py:299
  4.5 26.8 %all_to_all.5.arrived = f32[1568,1,128]{2,1,0:T(1,128)S(1)} all-to-all(f32[1568,1,128]{2,1,0:T(1,128)} %pack.1), channel_id=1, replica_groups=mesh['tile'=8,'wp'=4] {'tile','wp'}, dimensions={0} | all-to-all | bytes 1605632 | tf_op jit(solution)/shard_map/all_to_all | solution.py:320
  31.3 0.0 copy-start
  31.3 0.7 copy-done
  32.0 35.4 %grid.1 = (f32[2,1024,1024]{2,1,0:T(8,128)}, f32[2,8,8,128]{3,2,1,0:T(8,128)S(1)}) custom-call(f32[8,16]{1,0:T(8,128)S(1)} %bitcast.3, f32[1568,1,128]{2,1,0:T(1,128)S(1)} %all_to_all.5.arrived), custom_call_target="tpu_custom_call" | custom-call | tf_op jit(solution)/shard_map/grid/pallas_call | solution.py:331
  67.4 1.9 %collective-permute-start = (f32[2,8,8,128]{3,2,1,0:T(8,128)S(1)}, f32[2,8,8,128]{3,2,1,0:T(8,128)S(1)}, u32[]{:S(2)}, u32[]{:S(2)}) collective-permute-start(f32[2,8,8,128]{3,2,1,0:T(8,128)S(1)} %get-tuple-element.7), channel_id=1, source_target_pairs={{0,4},{4,8},{8,12},{12,16},{16,20},{20,24},{24,28},{1,5},{5,9},{9,... | collective-permute-start | bytes 196616 | tf_op jit(solution)/shard_map/ppermute | solution.py:285
  69.3 4.4 %collective-permute-done.edge = f32[2,8,8,128]{3,2,1,0:T(8,128)S(1)} collective-permute-done((f32[2,8,8,128]{3,2,1,0:T(8,128)S(1)}, f32[2,8,8,128]{3,2,1,0:T(8,128)S(1)}, u32[]{:S(2)}, u32[]{:S(2)}) %collective-permute-start) | collective-permute-done | bytes 65568 | tf_op jit(solution)/shard_map/ppermute | solution.py:285
  73.6 2.5 %edges.1 = f32[2,1024,1024]{2,1,0:T(8,128)} custom-call(f32[2,8,8,128]{3,2,1,0:T(8,128)S(1)} %collective-permute-done.edge, f32[2,1024,1024]{2,1,0:T(8,128)} %get-tuple-element.8.grid_in), custom_call_target="tpu_custom_call", output_to_operand_aliasing={{}: (1, {})} | custom-call | tf_op jit(solution)/shard_map/edges/pallas_call | solution.py:354
Async XLA Ops:
  31.3 0.7 copy-start
  67.4 6.3 %collective-permute-start = (f32[2,8,8,128]{3,2,1,0:T(8,128)S(1)}, f32[2,8,8,128]{3,2,1,0:T(8,128)S(1)}, u32[]{:S(2)}, u32[]{:S(2)}) collective-permute-start(f32[2,8,8,128]{3,2,1,0:T(8,128)S(1)} %get-tuple-element.7), channel_id=1, source_target_pairs={{0,4},{4,8},{8,12},{12,16},{16,20},{20,24},{24,28},{1,5},{5,9},{9,... | collective-permute-start | bytes 196616 | tf_op jit(solution)/shard_map/ppermute | solution.py:285

commit v4 on v3

--- a/solution.py
+++ b/solution.py
@@ -124,14 +124,13 @@
     last_lo = jnp.where(past, last_lo, zero)
     left_hi = jnp.concatenate(re_hi + im_hi + [last_hi], axis=0)
     left_lo = jnp.concatenate(re_lo + im_lo + [last_lo], axis=0)
-    left = jnp.concatenate([left_hi, left_lo], axis=1)
+    left = jnp.concatenate([left_hi, left_lo, left_hi], axis=1)
 
     v_hi, v_lo = split(twice(kv))
     hi_rows, lo_rows = spread(step_v, ROWS // 16, [v_hi, v_lo])
-    right = jnp.concatenate(hi_rows + lo_rows, axis=0)
-    right = jnp.concatenate([right, right], axis=1)
-    product = lax.dot_general(left, right, (((1,), (1,)), ((), ())), preferred_element_type=f32)
-    return product[:, :ROWS] + product[:, ROWS:]
+    right_hi = jnp.concatenate(hi_rows, axis=0)
+    right = jnp.concatenate([right_hi, right_hi, jnp.concatenate(lo_rows, axis=0)], axis=1)
+    return lax.dot_general(left, right, (((1,), (1,)), ((), ())), preferred_element_type=f32)
 
 
 def tap_table(kernel):

time: 76.5 us -> 74.2 us (0.970)
  the two profiles are of different devices: /device:TPU:9 before, /device:TPU:16 now
where the time goes in v4:
time: 74.2 us; the launch traced here: 73.5 us
  Pallas kernels  40.7 us (55%)
  blocking collectives  25.1 us (34%)
  waiting for transfers between devices  5.13 us (7%)
  starting transfers between devices  1.92 us (3%)
    pallas_call x1, Pallas kernels, shards(): pl.pallas_call(functools.partial(grid_kernel, peers, cap, with_low), out_...  33.6 us
    all_to_all x1, blocking collectives, shards(): lax.all_to_all(buckets, ('tile', 'wp'), split_axis=0, concat_axis=0, tile...  25.1 us
    ppermute x1, waiting for transfers between devices, shifted(): return lax.ppermute(block, axis, route)  5.13 us
    pallas_call x1, Pallas kernels, shards(): pl.pallas_call(functools.partial(pack_kernel, peers, cap), out_shape=jax....  4.49 us
    pallas_call x1, Pallas kernels, shards(): pl.pallas_call(edge_kernel, out_shape=jax.ShapeDtypeStruct((2, TILE, TILE...  2.52 us
    ppermute x1, starting transfers between devices, shifted(): return lax.ppermute(block, axis, route)  1.92 us
  transfers between devices with their start and end apart: 1, of which 1 were waited for; matrix products, arithmetic and copies ran while one was open for 0% of the time, Pallas kernels for 0%

profile of v4, /device:TPU:16, one launch (start us, length us, event | category | flops | bytes accessed | tf_op | source)
XLA Modules:
  0.0 73.5 jit_solution(14147624468364439289)
XLA Ops:
  0.0 4.5 %pack.1 = f32[1568,1,128]{2,1,0:T(1,128)} custom-call(s32[256]{0:T(256)} %bitcast.4, s32[256]{0:T(256)} %patch.1, f32[256,2,128]{2,1,0:T(2,128)} %vis.1, f32[256,128]{1,0:T(8,128)} %weight.1, s32[256,128]{1,0:T(8,128)} %cell.1, s32[256,128]{1,0:T(8,128)} %tap.1), custom_call_target="tpu_custom_call" | custom-call | tf_op jit(solution)/shard_map/pack/pallas_call | solution.py:298
  4.5 25.1 %all_to_all.5.arrived = f32[1568,1,128]{2,1,0:T(1,128)S(1)} all-to-all(f32[1568,1,128]{2,1,0:T(1,128)} %pack.1), channel_id=1, replica_groups=mesh['tile'=8,'wp'=4] {'tile','wp'}, dimensions={0} | all-to-all | bytes 1605632 | tf_op jit(solution)/shard_map/all_to_all | solution.py:319
  29.6 0.0 copy-start
  29.6 0.7 copy-done
  30.3 33.6 %grid.1 = (f32[2,1024,1024]{2,1,0:T(8,128)}, f32[2,8,8,128]{3,2,1,0:T(8,128)S(1)}) custom-call(f32[8,16]{1,0:T(8,128)S(1)} %bitcast.3, f32[1568,1,128]{2,1,0:T(1,128)S(1)} %all_to_all.5.arrived), custom_call_target="tpu_custom_call" | custom-call | tf_op jit(solution)/shard_map/grid/pallas_call | solution.py:330
  64.0 1.9 %collective-permute-start = (f32[2,8,8,128]{3,2,1,0:T(8,128)S(1)}, f32[2,8,8,128]{3,2,1,0:T(8,128)S(1)}, u32[]{:S(2)}, u32[]{:S(2)}) collective-permute-start(f32[2,8,8,128]{3,2,1,0:T(8,128)S(1)} %get-tuple-element.7), channel_id=1, source_target_pairs={{0,4},{4,8},{8,12},{12,16},{16,20},{20,24},{24,28},{1,5},{5,9},{9,... | collective-permute-start | bytes 196616 | tf_op jit(solution)/shard_map/ppermute | solution.py:284
  65.9 5.1 %collective-permute-done.edge = f32[2,8,8,128]{3,2,1,0:T(8,128)S(1)} collective-permute-done((f32[2,8,8,128]{3,2,1,0:T(8,128)S(1)}, f32[2,8,8,128]{3,2,1,0:T(8,128)S(1)}, u32[]{:S(2)}, u32[]{:S(2)}) %collective-permute-start) | collective-permute-done | bytes 65568 | tf_op jit(solution)/shard_map/ppermute | solution.py:284
  71.0 2.5 %edges.1 = f32[2,1024,1024]{2,1,0:T(8,128)} custom-call(f32[2,8,8,128]{3,2,1,0:T(8,128)S(1)} %collective-permute-done.edge, f32[2,1024,1024]{2,1,0:T(8,128)} %get-tuple-element.8.grid_in), custom_call_target="tpu_custom_call", output_to_operand_aliasing={{}: (1, {})} | custom-call | tf_op jit(solution)/shard_map/edges/pallas_call | solution.py:353
Async XLA Ops:
  29.6 0.7 copy-start
  64.0 7.1 %collective-permute-start = (f32[2,8,8,128]{3,2,1,0:T(8,128)S(1)}, f32[2,8,8,128]{3,2,1,0:T(8,128)S(1)}, u32[]{:S(2)}, u32[]{:S(2)}) collective-permute-start(f32[2,8,8,128]{3,2,1,0:T(8,128)S(1)} %get-tuple-element.7), channel_id=1, source_target_pairs={{0,4},{4,8},{8,12},{12,16},{16,20},{20,24},{24,28},{1,5},{5,9},{9,... | collective-permute-start | bytes 196616 | tf_op jit(solution)/shard_map/ppermute | solution.py:284

commit v5 on v3

--- a/solution.py
+++ b/solution.py
@@ -96,6 +96,19 @@
     return jnp.concatenate([x, x], axis=0)
 
 
+def look_up(table, index):
+    numbers = lax.GatherDimensionNumbers(
+        offset_dims=(),
+        collapsed_slice_dims=(1,),
+        start_index_map=(1,),
+        operand_batching_dims=(0,),
+        start_indices_batching_dims=(0,),
+    )
+    return lax.gather(
+        table, index[..., None], numbers, (1, 1), mode=lax.GatherScatterMode.PROMISE_IN_BOUNDS
+    )
+
+
 def spread(groups, count, values):
     zero = jnp.zeros((16, ROWS), bf16)
     picks = [groups == 2.0 * g for g in range(count)]
@@ -106,8 +119,8 @@
     sub = lax.broadcasted_iota(jnp.int32, (8, ROWS), 0)
     at_v = code & 127
     at_u = (code >> 7) & 127
-    ku = jnp.take_along_axis(table, at_u, axis=1)
-    kv = jnp.take_along_axis(table, at_v, axis=1)
+    ku = look_up(table, at_u)
+    kv = look_up(table, at_v)
     group_u = ((code >> 17) & 7) + jnp.where(sub < (at_u & 7), 1, 0)
     group_v = ((code >> 14) & 7) + jnp.where(sub < (at_v & 7), 1, 0) + 8 * parity
     step_u = jnp.concatenate([group_u, group_u - 1], axis=0).astype(f32).astype(bf16)
@@ -124,14 +137,14 @@
     last_lo = jnp.where(past, last_lo, zero)
     left_hi = jnp.concatenate(re_hi + im_hi + [last_hi], axis=0)
     left_lo = jnp.concatenate(re_lo + im_lo + [last_lo], axis=0)
-    left = jnp.concatenate([left_hi, left_lo], axis=1)
+    left = jnp.concatenate([left_hi, left_lo], axis=0)
+    left = jnp.concatenate([left, left], axis=1)
 
     v_hi, v_lo = split(twice(kv))
     hi_rows, lo_rows = spread(step_v, ROWS // 16, [v_hi, v_lo])
-    right = jnp.concatenate(hi_rows + lo_rows, axis=0)
-    right = jnp.concatenate([right, right], axis=1)
+    right = jnp.concatenate([jnp.concatenate(hi_rows, axis=0), jnp.concatenate(lo_rows, axis=0)], axis=1)
     product = lax.dot_general(left, right, (((1,), (1,)), ((), ())), preferred_element_type=f32)
-    return product[:, :ROWS] + product[:, ROWS:]
+    return product[:ROW_BLOCK] + product[ROW_BLOCK:]
 
 
 def tap_table(kernel):

time: 76.5 us -> 75.1 us (0.982)
  the two profiles are of different devices: /device:TPU:9 before, /device:TPU:0 now
where the time goes in v5:
time: 75.1 us; the launch traced here: 74.3 us
  Pallas kernels  41.7 us (56%)
  blocking collectives  28.3 us (38%)
  waiting for transfers between devices  1.88 us (3%)
  starting transfers between devices  1.7 us (2%)
    pallas_call x1, Pallas kernels, shards(): pl.pallas_call(functools.partial(grid_kernel, peers, cap, with_low), out_...  34.7 us
    all_to_all x1, blocking collectives, shards(): lax.all_to_all(buckets, ('tile', 'wp'), split_axis=0, concat_axis=0, tile...  28.3 us
    pallas_call x1, Pallas kernels, shards(): pl.pallas_call(functools.partial(pack_kernel, peers, cap), out_shape=jax....  4.49 us
    pallas_call x1, Pallas kernels, shards(): pl.pallas_call(edge_kernel, out_shape=jax.ShapeDtypeStruct((2, TILE, TILE...  2.52 us
    ppermute x1, waiting for transfers between devices, shifted(): return lax.ppermute(block, axis, route)  1.88 us
    ppermute x1, starting transfers between devices, shifted(): return lax.ppermute(block, axis, route)  1.7 us
  transfers between devices with their start and end apart: 1, of which 1 were waited for; matrix products, arithmetic and copies ran while one was open for 0% of the time, Pallas kernels for 0%

profile of v5, /device:TPU:0, one launch (start us, length us, event | category | flops | bytes accessed | tf_op | source)
XLA Modules:
  0.0 74.3 jit_solution(15543018412252186534)
XLA Ops:
  0.0 4.5 %pack.1 = f32[1568,1,128]{2,1,0:T(1,128)} custom-call(s32[256]{0:T(256)} %bitcast.4, s32[256]{0:T(256)} %patch.1, f32[256,2,128]{2,1,0:T(2,128)} %vis.1, f32[256,128]{1,0:T(8,128)} %weight.1, s32[256,128]{1,0:T(8,128)} %cell.1, s32[256,128]{1,0:T(8,128)} %tap.1), custom_call_target="tpu_custom_call" | custom-call | tf_op jit(solution)/shard_map/pack/pallas_call | solution.py:312
  4.5 28.3 %all_to_all.5.arrived = f32[1568,1,128]{2,1,0:T(1,128)S(1)} all-to-all(f32[1568,1,128]{2,1,0:T(1,128)} %pack.1), channel_id=1, replica_groups=mesh['tile'=8,'wp'=4] {'tile','wp'}, dimensions={0} | all-to-all | bytes 1605632 | tf_op jit(solution)/shard_map/all_to_all | solution.py:333
  32.8 0.0 copy-start
  32.8 0.7 copy-done
  33.5 34.7 %grid.1 = (f32[2,1024,1024]{2,1,0:T(8,128)}, f32[2,8,8,128]{3,2,1,0:T(8,128)S(1)}) custom-call(f32[8,16]{1,0:T(8,128)S(1)} %bitcast.3, f32[1568,1,128]{2,1,0:T(1,128)S(1)} %all_to_all.5.arrived), custom_call_target="tpu_custom_call" | custom-call | tf_op jit(solution)/shard_map/grid/pallas_call | solution.py:344
  68.2 1.7 %collective-permute-start = (f32[2,8,8,128]{3,2,1,0:T(8,128)S(1)}, f32[2,8,8,128]{3,2,1,0:T(8,128)S(1)}, u32[]{:S(2)}, u32[]{:S(2)}) collective-permute-start(f32[2,8,8,128]{3,2,1,0:T(8,128)S(1)} %get-tuple-element.7), channel_id=1, source_target_pairs={{0,4},{4,8},{8,12},{12,16},{16,20},{20,24},{24,28},{1,5},{5,9},{9,... | collective-permute-start | bytes 196616 | tf_op jit(solution)/shard_map/ppermute | solution.py:298
  69.9 1.9 %collective-permute-done.edge = f32[2,8,8,128]{3,2,1,0:T(8,128)S(1)} collective-permute-done((f32[2,8,8,128]{3,2,1,0:T(8,128)S(1)}, f32[2,8,8,128]{3,2,1,0:T(8,128)S(1)}, u32[]{:S(2)}, u32[]{:S(2)}) %collective-permute-start) | collective-permute-done | bytes 65568 | tf_op jit(solution)/shard_map/ppermute | solution.py:298
  71.8 2.5 %edges.1 = f32[2,1024,1024]{2,1,0:T(8,128)} custom-call(f32[2,8,8,128]{3,2,1,0:T(8,128)S(1)} %collective-permute-done.edge, f32[2,1024,1024]{2,1,0:T(8,128)} %get-tuple-element.8.grid_in), custom_call_target="tpu_custom_call", output_to_operand_aliasing={{}: (1, {})} | custom-call | tf_op jit(solution)/shard_map/edges/pallas_call | solution.py:367
Async XLA Ops:
  32.8 0.7 copy-start
  68.2 3.6 %collective-permute-start = (f32[2,8,8,128]{3,2,1,0:T(8,128)S(1)}, f32[2,8,8,128]{3,2,1,0:T(8,128)S(1)}, u32[]{:S(2)}, u32[]{:S(2)}) collective-permute-start(f32[2,8,8,128]{3,2,1,0:T(8,128)S(1)} %get-tuple-element.7), channel_id=1, source_target_pairs={{0,4},{4,8},{8,12},{12,16},{16,20},{20,24},{24,28},{1,5},{5,9},{9,... | collective-permute-start | bytes 196616 | tf_op jit(solution)/shard_map/ppermute | solution.py:298
